TPU v7x, 32 devices: a whole 2x2x4 slice. The times are simulated.
32 devices in a mesh: utt: 16 (over z, x, core), tm: 2 (over y).
Axes of the slice: x: 2, y: 2, z: 4, core: 2. Of those that a mesh axis runs over, the one named last changes fastest.
Arguments:
- noisy_mel: bfloat16 [2, 80, 65536], P('tm', None, 'utt'), may hold values from -6 to 6
- encoder_mean: bfloat16 [80, 65536], P(None, ('utt', 'tm')), may hold values from -6 to 6
- time_embedding: bfloat16 [2, 128, 1024], P('tm', 'utt'), may hold values from -6 to 6
- utter_lengths: int32 [16, 8], P('utt'), may hold values from 1 to 2049, as said below
- out_cotangent: bfloat16 [2, 256, 32768], P('tm', None, 'utt'), may hold values from -6 to 6
- conv_one: bfloat16 [3, 160, 256], replicated, may hold values from -0.25 to 0.25
- bias_one: bfloat16 [256], replicated, may hold values from -3 to 3
- gain_one: bfloat16 [256], replicated, may hold values from 0.099609375 to 1.8984375
- shift_one: bfloat16 [256], replicated, may hold values from -2 to 2
- time_weight: bfloat16 [1024, 256], replicated, may hold values from -0.25 to 0.25
- time_bias: bfloat16 [256], replicated, may hold values from -2 to 2
- conv_two: bfloat16 [3, 256, 256], replicated, may hold values from -0.21875 to 0.21875
- bias_two: bfloat16 [256], replicated, may hold values from -3 to 3
- gain_two: bfloat16 [256], replicated, may hold values from 0.099609375 to 1.8984375
- shift_two: bfloat16 [256], replicated, may hold values from -2 to 2
- skip_weight: bfloat16 [160, 256], replicated, may hold values from -0.5 to 0.5
- skip_bias: bfloat16 [256], replicated, may hold values from -2 to 2
- norm_gain: bfloat16 [256], replicated, may hold values from 0.099609375 to 1.8984375
- norm_shift: bfloat16 [256], replicated, may hold values from -2 to 2
- heads_input: bfloat16 [256, 384], replicated, may hold values from -0.5 to 0.5
- heads_output: bfloat16 [128, 256], replicated, may hold values from -2 to 2
- output_bias: bfloat16 [256], replicated, may hold values from -2 to 2
- feed_gain: bfloat16 [256], replicated, may hold values from 0.099609375 to 1.8984375
- feed_shift: bfloat16 [256], replicated, may hold values from -2 to 2
- expand_weight: bfloat16 [256, 1024], replicated, may hold values from -0.375 to 0.375
- expand_bias: bfloat16 [1024], replicated, may hold values from -2 to 2
- snake_alpha: bfloat16 [1024], replicated, may hold values from 0.5 to 2
- snake_beta: bfloat16 [1024], replicated, may hold values from 0.5 to 2
- reduce_weight: bfloat16 [1024, 256], replicated, may hold values from -0.1875 to 0.1875
- reduce_bias: bfloat16 [256], replicated, may hold values from -2 to 2
- down_weight: bfloat16 [3, 256, 256], replicated, may hold values from -0.21875 to 0.21875
- down_bias: bfloat16 [256], replicated, may hold values from -2 to 2
Outputs:
- down_output: bfloat16 [2, 256, 32768], P('tm', None, 'utt')
- grad_noisy: float32 [2, 80, 65536], P('tm', None, 'utt')
- grad_mean: float32 [80, 65536], P(None, ('utt', 'tm'))
- grad_time: float32 [2, 128, 1024], P('tm', 'utt')
- grad_conv_one: float32 [3, 160, 256], replicated
- grad_bias_one: float32 [256], replicated
- grad_gain_one: float32 [256], replicated
- grad_shift_one: float32 [256], replicated
- grad_time_weight: float32 [1024, 256], replicated
- grad_time_bias: float32 [256], replicated
- grad_conv_two: float32 [3, 256, 256], replicated
- grad_bias_two: float32 [256], replicated
- grad_gain_two: float32 [256], replicated
- grad_shift_two: float32 [256], replicated
- grad_skip_weight: float32 [160, 256], replicated
- grad_skip_bias: float32 [256], replicated
- grad_norm_gain: float32 [256], replicated
- grad_norm_shift: float32 [256], replicated
- grad_heads_input: float32 [256, 384], replicated
- grad_heads_output: float32 [128, 256], replicated
- grad_output_bias: float32 [256], replicated
- grad_feed_gain: float32 [256], replicated
- grad_feed_shift: float32 [256], replicated
- grad_expand_weight: float32 [256, 1024], replicated
- grad_expand_bias: float32 [1024], replicated
- grad_snake_alpha: float32 [1024], replicated
- grad_snake_beta: float32 [1024], replicated
- grad_reduce_weight: float32 [1024, 256], replicated
- grad_reduce_bias: float32 [256], replicated
- grad_down_weight: float32 [3, 256, 256], replicated
- grad_down_bias: float32 [256], replicated
Inputs may be any that keep to these rules, and one draw needn't show every extreme that they name: `utter_lengths`: each row lists one index of utt's utterances in the order of their frames; a row's lengths sum to at most 4096, the rest of its frames is padding, and some row sums to exactly 4096. Its longest utterance then has the most frames, which is reached in every draw.
All inputs are finite; a program needn't handle non-finite values.
Results may differ from a plain program's by a relative error of at most 0.025.
The roundings to bfloat16 on the way count: a program that leaves them out, or rounds other values in their place, can miss the bound.
Values may be sent and summed in bfloat16 or wider, within the bound.
A program may use at most 192 MiB of HBM per device.

v0:
```python
import jax
import jax.numpy as jnp
from jax import lax
from jax.sharding import PartitionSpec as P

HEADS = 2
GROUPS = 8


EPSILON = 1e-05
MASKED = -1e30


def mish_act(values):
    return values * jnp.tanh(jax.nn.softplus(values))


def pack_layout(lengths_row, frames):
    ends_at = jnp.cumsum(lengths_row)
    starts_at = ends_at - lengths_row
    used_frames = ends_at[-1]
    places = jnp.arange(frames, dtype=jnp.int32)
    segment = jnp.sum((places[:, None] >= ends_at[None, :]).astype(jnp.int32), axis=1)
    seg_rows = (
        jnp.arange(lengths_row.shape[0], dtype=jnp.int32)[:, None] == segment[None, :]
    ).astype(jnp.float32)
    frame_mask = (places < used_frames).astype(jnp.float32)
    joined = (segment[1:] == segment[:-1]).astype(jnp.float32)
    zero_one = jnp.zeros((1,), jnp.float32)
    same_prev = jnp.concatenate([zero_one, joined]) * frame_mask
    same_next = jnp.concatenate([joined, zero_one]) * frame_mask
    return (segment, starts_at, ends_at, used_frames, seg_rows, frame_mask, same_prev, same_next)


def segment_sums(values, seg_rows):
    return jnp.sum(values[:, None, :] * seg_rows[None], axis=2)


def segment_spread(statistic, seg_rows):
    return jnp.sum(statistic[:, :, None] * seg_rows[None], axis=1)


def group_norm(pre_act, gain_vec, shift_vec, seg_rows, counts):
    channels, frames = pre_act.shape
    per_group = channels // GROUPS

    def group_stat(values):
        grouped = jnp.sum(values.reshape(GROUPS, per_group, frames), axis=1)
        totals = segment_sums(grouped, seg_rows) / (counts[None, :] * per_group)
        per_frame = segment_spread(totals, seg_rows)
        return jnp.broadcast_to(per_frame[:, None, :], (GROUPS, per_group, frames)).reshape(
            channels, frames
        )

    centered = pre_act - group_stat(pre_act)
    scales = lax.rsqrt(group_stat(centered * centered) + EPSILON)
    return centered * scales * gain_vec[:, None] + shift_vec[:, None]


def layer_norm(values, gain_vec, shift_vec):
    centered = values - jnp.mean(values, axis=0, keepdims=True)
    spread = jnp.mean(centered * centered, axis=0, keepdims=True)
    return centered * lax.rsqrt(spread + EPSILON) * gain_vec[:, None] + shift_vec[:, None]


def snake_act(values, alpha_vec, beta_vec):
    return values + jnp.sin(alpha_vec[:, None] * values) ** 2 / beta_vec[:, None]


def shift_later(values):
    return jnp.concatenate([jnp.zeros_like(values[:, :1]), values[:, :-1]], axis=1)


def shift_earlier(values):
    return jnp.concatenate([values[:, 1:], jnp.zeros_like(values[:, :1])], axis=1)


def matmul_t(weight, inputs):
    return lax.dot_general(
        weight, inputs, (((0,), (0,)), ((), ())), preferred_element_type=jnp.float32
    )


def weight_grad(inputs, grad_low):
    return lax.dot_general(
        inputs, grad_low, (((1,), (1,)), ((), ())), preferred_element_type=jnp.float32
    )


def input_grad(weight, grad_low):
    return jnp.dot(weight, grad_low, preferred_element_type=jnp.float32)


def conv_taps(inputs, same_prev, same_next):
    before = shift_later(inputs) * same_prev.astype(inputs.dtype)[None]
    after = shift_earlier(inputs) * same_next.astype(inputs.dtype)[None]
    return (before, inputs, after)


def down_taps(inputs, same_prev, same_next):
    even_cols = inputs[:, 0::2]
    odd_cols = inputs[:, 1::2]
    before = shift_later(odd_cols) * same_prev[0::2].astype(inputs.dtype)[None]
    after = odd_cols * same_next[0::2].astype(inputs.dtype)[None]
    return (before, even_cols, after)


def conv_forward(weight, tap_list):
    return (
        matmul_t(weight[0], tap_list[0])
        + matmul_t(weight[1], tap_list[1])
        + matmul_t(weight[2], tap_list[2])
    )


def conv_backward(weight, tap_list, grad_low, same_prev, same_next):
    grad_weight = jnp.stack([weight_grad(one_tap, grad_low) for one_tap in tap_list])
    grad_input = (
        input_grad(weight[1], grad_low)
        + shift_earlier(input_grad(weight[0], grad_low) * same_prev[None])
        + shift_later(input_grad(weight[2], grad_low) * same_next[None])
    )
    return (grad_weight, grad_input)


def down_backward(weight, tap_list, grad_low, same_prev, same_next):
    grad_weight = jnp.stack([weight_grad(one_tap, grad_low) for one_tap in tap_list])
    grad_even = input_grad(weight[1], grad_low)
    grad_odd = input_grad(weight[2], grad_low) * same_next[0::2][None] + shift_earlier(
        input_grad(weight[0], grad_low) * same_prev[0::2][None]
    )
    grad_input = jnp.stack([grad_even, grad_odd], axis=2).reshape(grad_even.shape[0], -1)
    return (grad_weight, grad_input)


def key_range(segment, starts_at, ends_at, used_frames, first, block):
    last = jnp.minimum(first + block, used_frames) - 1
    key_low = starts_at[segment[first]] // block
    key_high = (ends_at[segment[last]] + block - 1) // block
    return (key_low, key_high)


def masked_scores(query_block, query_segs, keys_all, segment, start, block, scale):
    key_block = lax.dynamic_slice_in_dim(keys_all, start, block, 2)
    key_segs = lax.dynamic_slice_in_dim(segment, start, block, 0)
    raw = (
        jnp.einsum("hdq,hdk->hqk", query_block, key_block, preferred_element_type=jnp.float32)
        * scale
    )
    return (jnp.where((query_segs[:, None] == key_segs[None, :])[None], raw, MASKED), key_block)


def attention_forward(queries, keys_all, values_all, segment, starts_at, ends_at, used_frames):
    heads, head_size, frames = queries.shape
    block = min(512, frames)
    scale = head_size ** (-0.5)
    block_count = (used_frames + block - 1) // block

    def one_block(block_index, carry):
        attended, log_sums = carry
        first = block_index * block
        query_block = lax.dynamic_slice_in_dim(queries, first, block, 2)
        query_segs = lax.dynamic_slice_in_dim(segment, first, block, 0)
        key_low, key_high = key_range(segment, starts_at, ends_at, used_frames, first, block)

        def stats_step(key_index, state):
            top_now, total_now = state
            scores, key_block = masked_scores(
                query_block, query_segs, keys_all, segment, key_index * block, block, scale
            )
            top_new = jnp.maximum(top_now, jnp.max(scores, axis=2))
            total_new = total_now * jnp.exp(top_now - top_new) + jnp.sum(
                jnp.exp(scores - top_new[:, :, None]), axis=2
            )
            return (top_new, total_new)

        start_state = (
            jnp.full((heads, block), MASKED, jnp.float32),
            jnp.zeros((heads, block), jnp.float32),
        )
        top_all, total_all = lax.fori_loop(key_low, key_high, stats_step, start_state)
        lse_block = top_all + jnp.log(total_all)

        def value_step(key_index, accum):
            start = key_index * block
            scores, key_block = masked_scores(
                query_block, query_segs, keys_all, segment, start, block, scale
            )
            probs_low = jnp.exp(scores - lse_block[:, :, None]).astype(jnp.bfloat16)
            value_block = lax.dynamic_slice_in_dim(values_all, start, block, 2)
            return accum + jnp.einsum(
                "hqk,hdk->hdq", probs_low, value_block, preferred_element_type=jnp.float32
            )

        accum = lax.fori_loop(
            key_low, key_high, value_step, jnp.zeros((heads, head_size, block), jnp.float32)
        )
        attended = lax.dynamic_update_slice_in_dim(attended, accum, first, 2)
        log_sums = lax.dynamic_update_slice_in_dim(log_sums, lse_block, first, 1)
        return (attended, log_sums)

    start_carry = (
        jnp.zeros((heads, head_size, frames), jnp.float32),
        jnp.zeros((heads, frames), jnp.float32),
    )
    return lax.fori_loop(0, block_count, one_block, start_carry)


def attention_backward(
    queries,
    keys_all,
    values_all,
    attended,
    log_sums,
    grad_attended,
    segment,
    starts_at,
    ends_at,
    used_frames,
):
    heads, head_size, frames = queries.shape
    block = min(512, frames)
    scale = head_size ** (-0.5)
    block_count = (used_frames + block - 1) // block
    deltas = jnp.sum(grad_attended.astype(jnp.float32) * attended, axis=1)

    def one_block(block_index, carry):
        grad_queries, grad_keys, grad_values = carry
        first = block_index * block
        query_block = lax.dynamic_slice_in_dim(queries, first, block, 2)
        query_segs = lax.dynamic_slice_in_dim(segment, first, block, 0)
        grad_block = lax.dynamic_slice_in_dim(grad_attended, first, block, 2)
        lse_block = lax.dynamic_slice_in_dim(log_sums, first, block, 1)
        delta_block = lax.dynamic_slice_in_dim(deltas, first, block, 1)
        key_low, key_high = key_range(segment, starts_at, ends_at, used_frames, first, block)

        def key_step(key_index, state):
            grad_query_block, grad_keys_now, grad_values_now = state
            start = key_index * block
            scores, key_block = masked_scores(
                query_block, query_segs, keys_all, segment, start, block, scale
            )
            value_block = lax.dynamic_slice_in_dim(values_all, start, block, 2)
            probs = jnp.exp(scores - lse_block[:, :, None])
            grad_value_block = jnp.einsum(
                "hqk,hdq->hdk",
                probs.astype(jnp.bfloat16),
                grad_block,
                preferred_element_type=jnp.float32,
            )
            grad_probs = jnp.einsum(
                "hdq,hdk->hqk", grad_block, value_block, preferred_element_type=jnp.float32
            )
            grad_scores = (probs * (grad_probs - delta_block[:, :, None])).astype(jnp.bfloat16)
            grad_query_block = (
                grad_query_block
                + jnp.einsum(
                    "hqk,hdk->hdq", grad_scores, key_block, preferred_element_type=jnp.float32
                )
                * scale
            )
            grad_key_block = (
                jnp.einsum(
                    "hqk,hdq->hdk", grad_scores, query_block, preferred_element_type=jnp.float32
                )
                * scale
            )
            grad_keys_now = lax.dynamic_update_slice_in_dim(
                grad_keys_now,
                lax.dynamic_slice_in_dim(grad_keys_now, start, block, 2) + grad_key_block,
                start,
                2,
            )
            grad_values_now = lax.dynamic_update_slice_in_dim(
                grad_values_now,
                lax.dynamic_slice_in_dim(grad_values_now, start, block, 2) + grad_value_block,
                start,
                2,
            )
            return (grad_query_block, grad_keys_now, grad_values_now)

        start_state = (jnp.zeros((heads, head_size, block), jnp.float32), grad_keys, grad_values)
        grad_query_block, grad_keys, grad_values = lax.fori_loop(
            key_low, key_high, key_step, start_state
        )
        grad_queries = lax.dynamic_update_slice_in_dim(grad_queries, grad_query_block, first, 2)
        return (grad_queries, grad_keys, grad_values)

    zero_grad = jnp.zeros((heads, head_size, frames), jnp.float32)
    return lax.fori_loop(0, block_count, one_block, (zero_grad, zero_grad, zero_grad))


def sum_tail(parts):
    return lax.psum(
        (
            parts[0],
            parts[1],
            parts[2],
            parts[3],
            parts[4],
            parts[5],
            parts[6],
            parts[7],
            parts[8],
            parts[9],
            parts[10],
            parts[11],
            parts[12],
            parts[13],
            parts[14],
        ),
        ("utt", "tm"),
    )


def sum_head(parts):
    return lax.psum(
        (
            parts[0],
            parts[1],
            parts[2],
            parts[3],
            parts[4],
            parts[5],
            parts[6],
            parts[7],
            parts[8],
            parts[9],
            parts[10],
            parts[11],
        ),
        ("utt", "tm"),
    )


def shards(
    noisy_mel,
    encoder_mean,
    time_embedding,
    utter_lengths,
    out_cotangent,
    conv_one,
    bias_one,
    gain_one,
    shift_one,
    time_weight,
    time_bias,
    conv_two,
    bias_two,
    gain_two,
    shift_two,
    skip_weight,
    skip_bias,
    norm_gain,
    norm_shift,
    heads_input,
    heads_output,
    output_bias,
    feed_gain,
    feed_shift,
    expand_weight,
    expand_bias,
    snake_alpha,
    snake_beta,
    reduce_weight,
    reduce_bias,
    down_weight,
    down_bias,
):
    frames = noisy_mel.shape[2]
    mel_channels = noisy_mel.shape[1]
    lengths_row = utter_lengths[0]
    segment, starts_at, ends_at, used_frames, seg_rows, frame_mask, same_prev, same_next = (
        pack_layout(lengths_row, frames)
    )
    counts = lengths_row.astype(jnp.float32)
    mask_low = frame_mask.astype(jnp.bfloat16)[None]
    even_mask = frame_mask[0::2]

    def norm_block(pre_act, gain_vec, shift_vec):
        return (
            mish_act(group_norm(pre_act, gain_vec, shift_vec, seg_rows, counts)) * frame_mask[None]
        )

    mean_full = lax.all_gather(encoder_mean, "tm", axis=1, tiled=True)
    inputs = jnp.concatenate([noisy_mel[0], mean_full], axis=0) * mask_low
    taps_one = conv_taps(inputs, same_prev, same_next)
    pre_one = conv_forward(conv_one, taps_one) + bias_one[:, None]
    block_one_out, pull_one = jax.vjp(
        norm_block, pre_one, gain_one.astype(jnp.float32), shift_one.astype(jnp.float32)
    )
    time_act, time_pull = jax.vjp(mish_act, time_embedding[0].astype(jnp.float32))
    time_low = time_act.astype(jnp.bfloat16)
    time_proj = jnp.dot(time_low, time_weight, preferred_element_type=jnp.float32) + time_bias[None]
    hidden_one = block_one_out + segment_spread(time_proj.T, seg_rows)
    act_two = (hidden_one * frame_mask[None]).astype(jnp.bfloat16)
    taps_two = conv_taps(act_two, same_prev, same_next)
    pre_two = conv_forward(conv_two, taps_two) + bias_two[:, None]
    hidden_two, pull_two = jax.vjp(
        norm_block, pre_two, gain_two.astype(jnp.float32), shift_two.astype(jnp.float32)
    )
    resid_one = hidden_two + matmul_t(skip_weight, inputs) + skip_bias[:, None]
    normed_one, norm_pull_one = jax.vjp(
        layer_norm, resid_one, norm_gain.astype(jnp.float32), norm_shift.astype(jnp.float32)
    )
    normed_one_low = normed_one.astype(jnp.bfloat16)
    projected = matmul_t(heads_input, normed_one_low).astype(jnp.bfloat16)
    inner = heads_output.shape[0]
    head_size = inner // HEADS
    queries = projected[:inner].reshape(HEADS, head_size, frames)
    keys_all = projected[inner : 2 * inner].reshape(HEADS, head_size, frames)
    values_all = projected[2 * inner :].reshape(HEADS, head_size, frames)
    attended, log_sums = attention_forward(
        queries, keys_all, values_all, segment, starts_at, ends_at, used_frames
    )
    attended_low = attended.reshape(inner, frames).astype(jnp.bfloat16)
    resid_two = resid_one + matmul_t(heads_output, attended_low) + output_bias[:, None]
    normed_two, norm_pull_two = jax.vjp(
        layer_norm, resid_two, feed_gain.astype(jnp.float32), feed_shift.astype(jnp.float32)
    )
    normed_two_low = normed_two.astype(jnp.bfloat16)
    expanded = matmul_t(expand_weight, normed_two_low) + expand_bias[:, None]
    snaked, snake_pull = jax.vjp(
        snake_act, expanded, snake_alpha.astype(jnp.float32), snake_beta.astype(jnp.float32)
    )
    snaked_low = snaked.astype(jnp.bfloat16)
    resid_three = resid_two + matmul_t(reduce_weight, snaked_low) + reduce_bias[:, None]
    down_in = (resid_three * frame_mask[None]).astype(jnp.bfloat16)
    taps_down = down_taps(down_in, same_prev, same_next)
    down_pre = conv_forward(down_weight, taps_down) + down_bias[:, None]
    down_output = (down_pre * even_mask[None]).astype(jnp.bfloat16)
    grad_down = out_cotangent[0] * even_mask.astype(jnp.bfloat16)[None]
    grad_down_bias = jnp.sum(grad_down.astype(jnp.float32), axis=1)
    grad_down_weight, grad_down_in = down_backward(
        down_weight, taps_down, grad_down, same_prev, same_next
    )
    grad_three = grad_down_in * frame_mask[None]
    grad_reduce_low = grad_three.astype(jnp.bfloat16)
    grad_reduce_bias = jnp.sum(grad_reduce_low.astype(jnp.float32), axis=1)
    grad_reduce_weight = weight_grad(snaked_low, grad_reduce_low)
    grad_snaked = input_grad(reduce_weight, grad_reduce_low)
    grad_expanded, grad_snake_alpha, grad_snake_beta = snake_pull(grad_snaked)
    grad_expand_low = grad_expanded.astype(jnp.bfloat16)
    grad_expand_bias = jnp.sum(grad_expand_low.astype(jnp.float32), axis=1)
    grad_expand_weight = weight_grad(normed_two_low, grad_expand_low)
    grad_normed_two = input_grad(expand_weight, grad_expand_low)
    grad_resid_ln_two, grad_feed_gain, grad_feed_shift = norm_pull_two(grad_normed_two)
    grad_two = grad_three + grad_resid_ln_two
    grad_attn_low = grad_two.astype(jnp.bfloat16)
    grad_output_bias = jnp.sum(grad_attn_low.astype(jnp.float32), axis=1)
    grad_heads_output = weight_grad(attended_low, grad_attn_low)
    grad_attended = (
        input_grad(heads_output, grad_attn_low)
        .astype(jnp.bfloat16)
        .reshape(HEADS, head_size, frames)
    )
    grad_queries, grad_keys, grad_values = attention_backward(
        queries,
        keys_all,
        values_all,
        attended,
        log_sums,
        grad_attended,
        segment,
        starts_at,
        ends_at,
        used_frames,
    )
    grad_projected = jnp.concatenate([grad_queries, grad_keys, grad_values], axis=0)
    grad_projected = grad_projected.reshape(3 * inner, frames).astype(jnp.bfloat16)
    grad_heads_input = weight_grad(normed_one_low, grad_projected)
    grad_normed_one = input_grad(heads_input, grad_projected)
    grad_resid_ln_one, grad_norm_gain, grad_norm_shift = norm_pull_one(grad_normed_one)
    grad_one = grad_two + grad_resid_ln_one
    tail_sums = sum_tail(
        (
            grad_down_weight,
            grad_down_bias,
            grad_reduce_weight,
            grad_reduce_bias,
            grad_snake_alpha,
            grad_snake_beta,
            grad_expand_weight,
            grad_expand_bias,
            grad_feed_gain,
            grad_feed_shift,
            grad_heads_output,
            grad_output_bias,
            grad_heads_input,
            grad_norm_gain,
            grad_norm_shift,
        )
    )
    grad_skip_low = grad_one.astype(jnp.bfloat16)
    grad_skip_bias = jnp.sum(grad_skip_low.astype(jnp.float32), axis=1)
    grad_skip_weight = weight_grad(inputs, grad_skip_low)
    grad_inputs_skip = input_grad(skip_weight, grad_skip_low)
    grad_pre_two, grad_gain_two, grad_shift_two = pull_two(grad_one)
    grad_pre_two_low = grad_pre_two.astype(jnp.bfloat16)
    grad_bias_two = jnp.sum(grad_pre_two_low.astype(jnp.float32), axis=1)
    grad_conv_two, grad_act_two = conv_backward(
        conv_two, taps_two, grad_pre_two_low, same_prev, same_next
    )
    grad_hidden_one = grad_act_two * frame_mask[None]
    grad_time_low = segment_sums(grad_hidden_one, seg_rows).T.astype(jnp.bfloat16)
    grad_time_bias = jnp.sum(grad_time_low.astype(jnp.float32), axis=0)
    grad_time_weight = lax.dot_general(
        time_low, grad_time_low, (((0,), (0,)), ((), ())), preferred_element_type=jnp.float32
    )
    grad_time_act = lax.dot_general(
        grad_time_low, time_weight, (((1,), (1,)), ((), ())), preferred_element_type=jnp.float32
    )
    grad_time = time_pull(grad_time_act)[0]
    grad_pre_one, grad_gain_one, grad_shift_one = pull_one(grad_hidden_one)
    grad_pre_one_low = grad_pre_one.astype(jnp.bfloat16)
    grad_bias_one = jnp.sum(grad_pre_one_low.astype(jnp.float32), axis=1)
    grad_conv_one, grad_inputs_conv = conv_backward(
        conv_one, taps_one, grad_pre_one_low, same_prev, same_next
    )
    grad_inputs = (grad_inputs_conv + grad_inputs_skip) * frame_mask[None]
    grad_noisy = grad_inputs[:mel_channels][None]
    grad_mean = lax.psum_scatter(
        grad_inputs[mel_channels:].astype(jnp.bfloat16), "tm", scatter_dimension=1, tiled=True
    ).astype(jnp.float32)
    head_sums = sum_head(
        (
            grad_conv_one,
            grad_bias_one,
            grad_gain_one,
            grad_shift_one,
            grad_time_weight,
            grad_time_bias,
            grad_conv_two,
            grad_bias_two,
            grad_gain_two,
            grad_shift_two,
            grad_skip_weight,
            grad_skip_bias,
        )
    )
    return (
        down_output[None],
        grad_noisy,
        grad_mean,
        grad_time[None],
        head_sums[0],
        head_sums[1],
        head_sums[2],
        head_sums[3],
        head_sums[4],
        head_sums[5],
        head_sums[6],
        head_sums[7],
        head_sums[8],
        head_sums[9],
        head_sums[10],
        head_sums[11],
        tail_sums[13],
        tail_sums[14],
        tail_sums[12],
        tail_sums[10],
        tail_sums[11],
        tail_sums[8],
        tail_sums[9],
        tail_sums[6],
        tail_sums[7],
        tail_sums[4],
        tail_sums[5],
        tail_sums[2],
        tail_sums[3],
        tail_sums[0],
        tail_sums[1],
    )


def solution(mesh):
    return jax.shard_map(
        shards,
        mesh=mesh,
        in_specs=(
            P("tm", None, "utt"),
            P(None, ("utt", "tm")),
            P("tm", "utt", None),
            P("utt", None),
            P("tm", None, "utt"),
            P(),
            P(),
            P(),
            P(),
            P(),
            P(),
            P(),
            P(),
            P(),
            P(),
            P(),
            P(),
            P(),
            P(),
            P(),
            P(),
            P(),
            P(),
            P(),
            P(),
            P(),
            P(),
            P(),
            P(),
            P(),
            P(),
            P(),
        ),
        out_specs=(
            P("tm", None, "utt"),
            P("tm", None, "utt"),
            P(None, ("utt", "tm")),
            P("tm", "utt", None),
            P(),
            P(),
            P(),
            P(),
            P(),
            P(),
            P(),
            P(),
            P(),
            P(),
            P(),
            P(),
            P(),
            P(),
            P(),
            P(),
            P(),
            P(),
            P(),
            P(),
            P(),
            P(),
            P(),
            P(),
            P(),
            P(),
            P(),
        ),
        check_vma=False,
    )
```

profile of v0, /device:TPU:0, one launch (start us, length us, event | category | flops | bytes accessed | tf_op | source)
XLA Modules:
  0.0 1142.4 jit_solution(6219968672513744075)
XLA Ops:
  15.6 11.6 %all_gather.3 = bf16[80,4096]{1,0:T(8,128)(2,1)S(1)} all-gather(bf16[80,2048]{1,0:T(8,128)(2,1)} %param.44), channel_id=1, replica_groups=mesh['utt'=16,'tm'=2] {'tm'}, dimensions={1}, use_global_device_ids=true | all-gather | bytes 983040 | tf_op jit(solution)/shard_map/all_gather | solution.py:385
  36.6 17.8 %multiply_reduce_fusion.1 = f32[256,4096]{1,0:T(8,128)} fusion(f32[8,4096]{1,0:T(8,128)S(1)} %fusion.155, f32[256,8]{1,0:T(8,128)S(1)} %copy.82), kind=kLoop, calls=%fused_computation.56 | loop fusion | flops 15728640 | bytes 4333568 | tf_op jit(solution)/shard_map/reduce_sum | solution.py:40
  54.8 6.2 fusion.95
  69.8 3.7 fusion.231
  78.8 139.5 %while.146 = (s32[]{:T(128)}, f32[2,64,4096]{2,1,0:T(8,128)S(1)}, f32[2,4096]{1,0:T(2,128)S(1)}, s32[]{:T(128)}, s32[4096]{0:T(1024)S(1)}, /*index=5*/s32[8]{0:T...) while((s32[]{:T(128)}, f32[2,64,4096]{2,1,0:T(8,128)S(1)}, ...), condition=%wide.region_24.26_spmd, body=%wide.region_17.25_spmd.sunk | while | flops 207686720 | bytes 7838067 | solution.py:206
  89.5 4.8 while.149
  94.4 4.6 while.150
  109.6 7.2 while.149
  116.9 6.9 while.150
  134.4 7.2 while.149
  141.7 6.9 while.150
  159.2 7.2 while.149
  166.5 6.9 while.150
  184.0 7.2 while.149
  191.3 6.9 while.150
  208.8 4.8 while.149
  213.7 4.6 while.150
  218.5 4.0 fusion.232
  233.9 12.2 %copy.84 = f32[256,2048,2]{0,2,1:T(2,128)} copy(f32[256,2048,2]{0,1,2:T(8,128)S(1)} %get-tuple-element.1098) | data formatting | bytes 8388608 | tf_op jit(solution)/shard_map/stack | solution.py:132
  246.1 6.1 reshape.571
  252.2 5.7 copy.85
  257.9 5.0 fusion.214
  263.0 75.3 %fusion.40 = (f32[1024]{0:T(1024)}, f32[1024]{0:T(1024)}, f32[1024]{0:T(1024)}, bf16[1024,4096]{0,1:T(8,128)(2,1)}, bf16[1024,4096]{0,1:T(8,128)(2,1)}) fusion(f32[4096,1024]{1,0:T(8,128)S(1)} %fusion.214, f32[1024]{0:T(1024)S(1)} %multiply_divide_fusion, f32[1024]{0:T(1024)S(1)} %convert_element_type.270, f32[1024]{0:T(1024)S(1)} %convert_element_type.269, ...), kind=kOutput, calls=%fused_computation.64 | convolution fusion | flops 2233463808 | bytes 38318080 | tf_op jit(solution)/shard_map/dot_general | solution.py:91
  338.3 6.2 multiply_reduce_fusion.5
  344.5 2.5 fusion.86
  348.2 3.2 convert_reduce_fusion.2
  355.2 183.7 %while.148 = (s32[]{:T(128)}, bf16[2,64,4096]{2,1,0:T(8,128)(2,1)}, f32[2,64,4096]{2,1,0:T(8,128)S(1)}, f32[2,64,4096]{2,1,0:T(8,128)}, s32[]{:T(128)}, /*index=...) while((s32[]{:T(128)}, bf16[2,64,4096]{2,1,0:T(8,128)(2,1)}, ...), condition=%wide.region_33.35_spmd, body=%wide.region_30.34_spmd.sunk | while | flops 339804224 | bytes 13800612 | solution.py:290
  365.9 14.4 %while.151 = (s32[]{:T(128)}, f32[2,64,512]{2,1,0:T(8,128)S(1)}, f32[2,64,4096]{2,1,0:T(8,128)S(1)}, f32[2,64,4096]{2,1,0:T(8,128)}, s32[]{:T(128)}, /*index=5*/...) while((s32[]{:T(128)}, f32[2,64,512]{2,1,0:T(8,128)S(1)}, ...), condition=%wide.region_32.33_spmd, body=%wide.region_31.32_spmd.sunk | while | flops 339804160 | bytes 12468451 | solution.py:283
  391.7 21.6 %while.151 = (s32[]{:T(128)}, f32[2,64,512]{2,1,0:T(8,128)S(1)}, f32[2,64,4096]{2,1,0:T(8,128)S(1)}, f32[2,64,4096]{2,1,0:T(8,128)}, s32[]{:T(128)}, /*index=5*/...) while((s32[]{:T(128)}, f32[2,64,512]{2,1,0:T(8,128)S(1)}, ...), condition=%wide.region_32.33_spmd, body=%wide.region_31.32_spmd.sunk | while | flops 339804160 | bytes 12468451 | solution.py:283
  424.8 21.6 %while.151 = (s32[]{:T(128)}, f32[2,64,512]{2,1,0:T(8,128)S(1)}, f32[2,64,4096]{2,1,0:T(8,128)S(1)}, f32[2,64,4096]{2,1,0:T(8,128)}, s32[]{:T(128)}, /*index=5*/...) while((s32[]{:T(128)}, f32[2,64,512]{2,1,0:T(8,128)S(1)}, ...), condition=%wide.region_32.33_spmd, body=%wide.region_31.32_spmd.sunk | while | flops 339804160 | bytes 12468451 | solution.py:283
  457.8 21.6 %while.151 = (s32[]{:T(128)}, f32[2,64,512]{2,1,0:T(8,128)S(1)}, f32[2,64,4096]{2,1,0:T(8,128)S(1)}, f32[2,64,4096]{2,1,0:T(8,128)}, s32[]{:T(128)}, /*index=5*/...) while((s32[]{:T(128)}, f32[2,64,512]{2,1,0:T(8,128)S(1)}, ...), condition=%wide.region_32.33_spmd, body=%wide.region_31.32_spmd.sunk | while | flops 339804160 | bytes 12468451 | solution.py:283
  490.8 21.6 %while.151 = (s32[]{:T(128)}, f32[2,64,512]{2,1,0:T(8,128)S(1)}, f32[2,64,4096]{2,1,0:T(8,128)S(1)}, f32[2,64,4096]{2,1,0:T(8,128)}, s32[]{:T(128)}, /*index=5*/...) while((s32[]{:T(128)}, f32[2,64,512]{2,1,0:T(8,128)S(1)}, ...), condition=%wide.region_32.33_spmd, body=%wide.region_31.32_spmd.sunk | while | flops 339804160 | bytes 12468451 | solution.py:283
  523.8 14.4 %while.151 = (s32[]{:T(128)}, f32[2,64,512]{2,1,0:T(8,128)S(1)}, f32[2,64,4096]{2,1,0:T(8,128)S(1)}, f32[2,64,4096]{2,1,0:T(8,128)}, s32[]{:T(128)}, /*index=5*/...) while((s32[]{:T(128)}, f32[2,64,512]{2,1,0:T(8,128)S(1)}, ...), condition=%wide.region_32.33_spmd, body=%wide.region_31.32_spmd.sunk | while | flops 339804160 | bytes 12468451 | solution.py:283
  551.3 6.9 convert_reduce_fusion.3
  568.7 8.6 fusion.216
  590.0 8.6 fusion.63
  598.6 37.3 %slice.125 = bf16[256,2048]{1,0:T(8,128)(2,1)} slice(bf16[256,4096]{1,0:T(8,128)(2,1)} %fusion.63), slice={[0:256:1], [1:4096:2]} | slice | bytes 2097152 | tf_op jit(solution)/shard_map/slice | solution.py:102
  635.9 37.5 %slice.129 = bf16[256,2048]{1,0:T(8,128)(2,1)} slice(bf16[256,4096]{1,0:T(8,128)(2,1)} %fusion.63), slice={[0:256:1], [0:4096:2]} | slice | bytes 2097152 | tf_op jit(solution)/shard_map/slice | solution.py:101
  673.4 3.1 fusion.110
  676.6 2.8 fusion.111
  686.7 7.1 fusion.127
  693.8 3.4 multiply_reduce_fusion
  705.0 3.6 fusion.213
  709.4 3.1 reduce_sum.561
  712.5 3.0 reduce_sum.567
  724.5 300.0 %all-reduce.10 = (f32[256]{0:T(256)}, f32[256]{0:T(256)}, f32[256]{0:T(256)}, f32[256]{0:T(256)}, f32[256]{0:T(256)}, /*index=5*/f32[256]{0:T(256)}, f32[256]{0:...) all-reduce(f32[256]{0:T(256)} %get-tuple-element.1073, ...), channel_id=1, replica_groups=mesh['utt'=16,'tm'=2] {'utt','tm'}, use_global_device_ids=true, to_apply=%region_52.54 | all-reduce | flops 6912 | bytes 55296 | tf_op jit(solution)/shard_map/psum | solution.py:317
  1026.2 2.5 slice_bitcast_fusion
  1030.5 92.7 %all-reduce.14.cloned.1.call-done = (f32[3,160,256]{2,1,0:T(8,128)}, f32[1024,256]{1,0:T(8,128)}, f32[3,256,256]{2,1,0:T(8,128)}, f32[160,256]{1,0:T(8,128)}, f3...) async-done(((f32[3,160,256]{2,1,0:T(8,128)}, f32[1024,256]{1,0:T(8,128)}, ...) | async-done | bytes 5898256 | tf_op jit(solution)/shard_map/psum | solution.py:317
  (839 shorter events, 347.0 us)
Async XLA Ops:
  8.0 254.9 %copy-start = (bf16[1024,256]{1,0:T(8,128)(2,1)S(1)}, bf16[1024,256]{1,0:T(8,128)(2,1)}, u32[]{:S(2)}) copy-start(bf16[1024,256]{1,0:T(8,128)(2,1)} %param.71) | copy-start | bytes 1572868
  8.1 1020.6 %reduce-scatter.2.cloned.1.call-start = ((), (), s32[]{:S(2)}) async-start(), calls=%async_computation.1 | async-start | bytes 983040 | tf_op jit(solution)/shard_map/reduce_scatter | solution.py:522
  9.8 58.6 %copy-start.19 = (f32[8,4096]{1,0:T(8,128)}, f32[8,4096]{1,0:T(8,128)S(1)}, u32[]{:S(2)}) copy-start(f32[8,4096]{1,0:T(8,128)S(1)} %fusion.155) | copy-start | bytes 393220
  10.5 57.9 %copy-start.114 = (f32[8]{0:T(128)}, f32[8]{0:T(128)S(1)}, u32[]{:S(2)}) copy-start(f32[8]{0:T(128)S(1)} %multiply_bitcast_fusion) | copy-start | bytes 100
  28.5 41.1 %copy-start.21 = (bf16[160,4096]{1,0:T(8,128)(2,1)}, bf16[160,4096]{1,0:T(8,128)(2,1)S(1)}, u32[]{:S(2)}) copy-start(bf16[160,4096]{1,0:T(8,128)(2,1)S(1)} %maximum_multiply_fusion) | copy-start | bytes 3932164
  29.9 32.2 %copy-start.89 = (bf16[4096]{0:T(1024)(128)(2,1)}, bf16[4096]{0:T(1024)(128)(2,1)S(1)}, u32[]{:S(2)}) copy-start(bf16[4096]{0:T(1024)(128)(2,1)S(1)} %get-tuple-element.1106) | copy-start | bytes 24580
  29.9 35.6 %copy-start.108 = (bf16[4096]{0:T(1024)(128)(2,1)}, bf16[4096]{0:T(1024)(128)(2,1)S(1)}, u32[]{:S(2)}) copy-start(bf16[4096]{0:T(1024)(128)(2,1)S(1)} %get-tuple-element.1077) | copy-start | bytes 24580
  29.9 195.2 %copy-start.87 = (f32[4096]{0:T(1024)}, f32[4096]{0:T(1024)S(1)}, u32[]{:S(2)}) copy-start(f32[4096]{0:T(1024)S(1)} %get-tuple-element.1107) | copy-start | bytes 49156
  29.9 199.5 %copy-start.85 = (f32[4096]{0:T(1024)}, f32[4096]{0:T(1024)S(1)}, u32[]{:S(2)}) copy-start(f32[4096]{0:T(1024)S(1)} %get-tuple-element.1078) | copy-start | bytes 49156
  33.5 21.3 %copy-start.47 = (f32[8,4096]{1,0:T(8,128)}, f32[8,4096]{1,0:T(8,128)S(1)}, u32[]{:S(2)}) copy-start(f32[8,4096]{1,0:T(8,128)S(1)} %multiply_reduce_fusion.23) | copy-start | bytes 393220
  34.9 19.6 %copy-start.135 = (bf16[256]{0:T(256)(128)(2,1)S(1)}, bf16[256]{0:T(256)(128)(2,1)}, u32[]{:S(2)}) copy-start(bf16[256]{0:T(256)(128)(2,1)} %param.50) | copy-start | bytes 1540
  34.9 19.6 %copy-start.136 = (bf16[256]{0:T(256)(128)(2,1)S(1)}, bf16[256]{0:T(256)(128)(2,1)}, u32[]{:S(2)}) copy-start(bf16[256]{0:T(256)(128)(2,1)} %param.51) | copy-start | bytes 1540
  36.3 24.8 %copy-start.53 = (f32[8,4096]{1,0:T(8,128)}, f32[8,4096]{1,0:T(8,128)S(1)}, u32[]{:S(2)}) copy-start(f32[8,4096]{1,0:T(8,128)S(1)} %broadcast_add_fusion.1) | copy-start | bytes 393220
  54.4 6.6 copy-start.116
  54.5 6.6 copy-start.124
  54.8 170.2 %copy-start.102 = (f32[2048]{0:T(1024)}, f32[2048]{0:T(1024)S(1)}, u32[]{:S(2)}) copy-start(f32[2048]{0:T(1024)S(1)} %slice.133) | copy-start | bytes 24580
  78.8 139.7 %copy-start.143 = (bf16[256]{0:T(256)(128)(2,1)S(1)}, bf16[256]{0:T(256)(128)(2,1)}, u32[]{:S(2)}) copy-start(bf16[256]{0:T(256)(128)(2,1)} %param.64) | copy-start | bytes 1540
  78.8 139.7 %copy-start.91 = (bf16[128,256]{1,0:T(8,128)(2,1)S(1)}, bf16[128,256]{1,0:T(8,128)(2,1)}, u32[]{:S(2)}) copy-start(bf16[128,256]{1,0:T(8,128)(2,1)} %param.63) | copy-start | bytes 196612
  222.6 124.3 %copy-start.73 = (f32[4096]{0:T(1024)}, f32[4096]{0:T(1024)S(1)}, u32[]{:S(2)}) copy-start(f32[4096]{0:T(1024)S(1)} %broadcast_multiply_fusion) | copy-start | bytes 49156
  225.0 122.0 %copy-start.82 = (f32[4096]{0:T(1024)}, f32[4096]{0:T(1024)S(1)}, u32[]{:S(2)}) copy-start(f32[4096]{0:T(1024)S(1)} %fusion.194) | copy-start | bytes 49156
  225.0 121.9 %copy-start.112 = (f32[256]{0:T(256)}, f32[256]{0:T(256)S(1)}, u32[]{:S(2)}) copy-start(f32[256]{0:T(256)S(1)} %convert_element_type.266) | copy-start | bytes 3076
  225.1 32.8 %copy-start.127 = (f32[256]{0:T(256)}, f32[256]{0:T(256)S(1)}, u32[]{:S(2)}) copy-start(f32[256]{0:T(256)S(1)} %convert_element_type.267) | copy-start | bytes 3076
  263.0 75.3 %copy-start.4 = (f32[256,4096]{1,0:T(8,128)S(1)}, f32[256,4096]{1,0:T(8,128)}, u32[]{:S(2)}) copy-start(f32[256,4096]{1,0:T(8,128)} %copy-done.3) | copy-start | bytes 12582916
  551.2 6.9 copy-start.7
  551.2 6.9 copy-start.56
  551.3 6.9 copy-start.60
  558.1 28.7 %copy-start.26 = (bf16[256,4096]{1,0:T(8,128)(2,1)}, bf16[256,4096]{1,0:T(8,128)(2,1)S(1)}, u32[]{:S(2)}) copy-start(bf16[256,4096]{1,0:T(8,128)(2,1)S(1)} %get-tuple-element.1068) | copy-start | bytes 6291460
  589.9 533.3 %all-reduce.14.cloned.1.call-start = ((), (), s32[]{:S(2)}) async-start(), calls=%async_computation.2 | async-start | bytes 11796480 | tf_op jit(solution)/shard_map/psum | solution.py:317
  589.9 109.7 %copy-start.120 = (bf16[2048]{0:T(1024)(128)(2,1)}, bf16[2048]{0:T(1024)(128)(2,1)S(1)}, u32[]{:S(2)}) copy-start(bf16[2048]{0:T(1024)(128)(2,1)S(1)} %convert_element_type.275) | copy-start | bytes 12292
  590.0 109.2 %copy-start.122 = (bf16[2048]{0:T(1024)(128)(2,1)}, bf16[2048]{0:T(1024)(128)(2,1)S(1)}, u32[]{:S(2)}) copy-start(bf16[2048]{0:T(1024)(128)(2,1)S(1)} %convert_element_type.276) | copy-start | bytes 12292
  598.6 74.8 %copy-start.109 = (bf16[4096]{0:T(1024)(128)(2,1)S(1)}, bf16[4096]{0:T(1024)(128)(2,1)}, u32[]{:S(2)}) copy-start(bf16[4096]{0:T(1024)(128)(2,1)} %copy-done.108) | copy-start | bytes 24580
  635.9 40.6 %copy-start.90 = (bf16[4096]{0:T(1024)(128)(2,1)S(1)}, bf16[4096]{0:T(1024)(128)(2,1)}, u32[]{:S(2)}) copy-start(bf16[4096]{0:T(1024)(128)(2,1)} %copy-done.89) | copy-start | bytes 24580
  673.4 6.0 copy-start.11
  686.7 7.2 copy-start.35
  686.7 18.3 %slice-start = ((s8[8388608]{0:T(1024)(128)(4,1)}), s8[4194304]{0:T(1024)(128)(4,1)S(1)}, s32[]{:S(2)}) async-start(s8[8388608]{0:T(1024)(128)(4,1)} %bitcast.596), calls=%async_computation.3 | async-start | bytes 8388608
  697.3 11.4 copy-start.68
  697.3 7.7 slice-start.1
  709.4 6.1 copy-start.126
  709.4 6.7 copy-start.147
  709.4 6.7 copy-start.67
  709.4 6.7 copy-start.121
  718.9 305.6 %copy-start.63 = (bf16[1024,256]{1,0:T(8,128)(2,1)S(1)}, bf16[1024,256]{1,0:T(8,128)(2,1)}, u32[]{:S(2)}) copy-start(bf16[1024,256]{1,0:T(8,128)(2,1)} %param.52) | copy-start | bytes 1572868
  1123.2 6.4 copy-start.92
  1123.2 7.1 copy-start.84
  1123.2 7.8 copy-start.97
  1123.2 8.5 copy-start.70
  1123.2 9.4 copy-start.69
  1125.2 8.4 copy-start.75
  (104 other events, 294.5 us)
Sparse Core Ops, SparseCore 0:
  590.0 272.7 reduce-scatter.1
Sparse Core Ops, SparseCore 1:
  708.8 414.4 all-reduce.13
where the time goes:
time: 1160 us; the launch traced here: 1140 us
  matrix products  332 us (29%)
  blocking collectives  312 us (27%)
  local copies, waits for them, and re-layouts  187 us (16%)
  other arithmetic  104 us (9%)
  loops' own time  97 us (8%)
  waiting for transfers between devices  92.7 us (8%)
  between operations  18.8 us (2%)
    psum x1, blocking collectives, sum_head(): lax.psum((parts[0], parts[1], parts[2], parts[3], parts[4], parts[5], par...  300 us
    dot_general x14, matrix products, input_grad(): return jnp.dot(weight, grad_low, preferred_element_type=jnp.float32)  103 us
    psum x1, waiting for transfers between devices, sum_head(): lax.psum((parts[0], parts[1], parts[2], parts[3], parts[4], parts[5], par...  92.7 us
    dot_general x32, matrix products, masked_scores(): jnp.einsum('hdq,hdk->hqk', query_block, key_block, preferred_element_type...  51.4 us
    another operation x1, loops' own time, attention_forward(): return lax.fori_loop(0, block_count, one_block, start_carry)  47.4 us
    another operation x1, loops' own time, attention_backward(): lax.fori_loop(0, block_count, one_block, (zero_grad, zero_grad, zero_grad))  47.1 us
    slice x1, local copies, waits for them, and re-layouts, down_taps(): even_cols = inputs[:, 0::2]  37.5 us
    slice x1, local copies, waits for them, and re-layouts, down_taps(): odd_cols = inputs[:, 1::2]  37.3 us
  transfers between devices with their start and end apart: 2, of which 1 were waited for; matrix products, arithmetic and copies ran while one was open for 12% of the time, Pallas kernels for 0%

commit v1 on v0

v1 whole, which is shorter than its diff:
```python
import functools

import jax
import jax.numpy as jnp
import numpy as np
from jax import lax
from jax.experimental import pallas as pl
from jax.experimental.pallas import tpu as pltpu
from jax.sharding import PartitionSpec as P

GROUPS = 8
EPSILON = 1e-05
BIG = 1e30
TILE = 256


def split_three(row):
    top = row.astype(jnp.bfloat16)
    rest = row - top.astype(jnp.float32)
    mid = rest.astype(jnp.bfloat16)
    last = (rest - mid.astype(jnp.float32)).astype(jnp.bfloat16)
    return (top, mid, last)


def segment_of(places, lens_ref, segs):
    segment = jnp.zeros(places.shape, jnp.int32)
    end = jnp.int32(0)
    for index in range(segs):
        end = end + lens_ref[index]
        segment = segment + (places >= end).astype(jnp.int32)
    return segment


def used_of(lens_ref, segs):
    total = jnp.int32(0)
    for index in range(segs):
        total = total + lens_ref[index]
    return total


def key_bounds(first, used, lens_ref, segs):
    last = jnp.minimum(first + TILE, used) - 1
    low = jnp.int32(0)
    high = used
    end = jnp.int32(0)
    for index in range(segs):
        start = end
        end = end + lens_ref[index]
        low = jnp.where(start <= first, start, low)
        high = jnp.where((start <= last) & (last < end), end, high)
    high = jnp.where(first + TILE > used, first + TILE, high)
    low = low // 128 * 128
    return (low, (high - low + TILE - 1) // TILE)


def fill_keys(kx_ref, rows_ref, row_at, lens_ref, segs, tail):
    tiles = rows_ref.shape[1] // TILE

    def step(index, carry):
        at = pl.multiple_of(index * TILE, TILE)
        source = pl.multiple_of(jnp.minimum(index, tiles - 1) * TILE, TILE)
        rows = rows_ref[row_at : row_at + 128, pl.ds(source, TILE)].astype(jnp.float32)
        rows = jnp.where(index < tiles, rows, 0.0)
        kx_ref[pl.ds(at, TILE), 0:128] = rows.T.astype(jnp.bfloat16)
        lane = lax.broadcasted_iota(jnp.int32, (TILE, 128), 1)
        if tail == "segments":
            place = lax.broadcasted_iota(jnp.int32, (TILE, 128), 0) + at
            segment = segment_of(place, lens_ref, segs)
            hot = (lane == segment) | ((lane >= 16) & (lane < 19))
        else:
            hot = lane < 3
        kx_ref[pl.ds(at, TILE), 128:256] = hot.astype(jnp.float32).astype(jnp.bfloat16)
        return carry

    lax.fori_loop(0, tiles + 1, step, 0)


def copy_padded(padded_ref, rows_ref, row_at):
    frames = rows_ref.shape[1]
    padded_ref[:, 0:frames] = rows_ref[row_at : row_at + 128, :]
    padded_ref[:, frames : frames + TILE] = jnp.zeros((128, TILE), padded_ref.dtype)


def query_tail(first, lens_ref, segs):
    row = lax.broadcasted_iota(jnp.int32, (16, TILE), 0)
    place = lax.broadcasted_iota(jnp.int32, (16, TILE), 1) + first
    segment = segment_of(place, lens_ref, segs)
    return jnp.where(row == segment, 0.0, -BIG).astype(jnp.bfloat16)


def three_rows(row):
    top, mid, last = split_three(row)
    at = lax.broadcasted_iota(jnp.int32, (16, row.shape[1]), 0)
    parts = jnp.where(
        at == 0,
        top.astype(jnp.float32),
        jnp.where(at == 1, mid.astype(jnp.float32), jnp.where(at == 2, last.astype(jnp.float32), 0.0)),
    )
    return parts.astype(jnp.bfloat16)


def fold_heads(rows, extra_one, extra_two):
    blank = jnp.zeros((64, TILE), jnp.bfloat16)
    fill_one = jnp.zeros((128 - extra_one.shape[0], TILE), jnp.bfloat16)
    left = jnp.concatenate([rows[0:64], blank, extra_one, fill_one], axis=0)
    right = jnp.concatenate([blank, rows[64:128], extra_two, fill_one], axis=0)
    return jnp.concatenate([left, right], axis=1)


def row_eights(values):
    return values.reshape(values.shape[0] // 8, 8, values.shape[1])


def by_tiles(widths, low, tiles, step, state):
    done = jnp.int32(0)
    for width in widths:
        end = done + (tiles - done) // width

        def wide_step(index, carry, width=width, start=done):
            place = start + (index - start) * width
            return step(pl.multiple_of(low + place * TILE, 128), width * TILE, place, carry)

        state = lax.fori_loop(done, end, wide_step, state)
        done = done + (end - done) * width
    return state


def scores_are_small(proj_ref):
    within = jnp.bool_(True)
    for head in range(2):
        norms = []
        for at in (64 * head, 128 + 64 * head):
            rows = proj_ref[at : at + 64, :].astype(jnp.float32)
            norms.append(jnp.max(jnp.sum(rows * rows, axis=0, keepdims=True)))
        within = within & (norms[0] * norms[1] <= 480.0 * 480.0)
    return within


def attn_forward_kernel(segs, lens_ref, proj_ref, att_ref, lse_ref, kx_ref, v_ref, score_ref):
    used = used_of(lens_ref, segs)
    small = scores_are_small(proj_ref)
    count = (used + TILE - 1) // TILE
    fill_keys(kx_ref, proj_ref, 128, lens_ref, segs, "segments")
    copy_padded(v_ref, proj_ref, 256)
    att_ref[...] = jnp.zeros_like(att_ref)
    lse_ref[...] = jnp.zeros_like(lse_ref)

    def query_step(index, carry):
        first = pl.multiple_of(index * TILE, TILE)
        queries = proj_ref[0:128, pl.ds(first, TILE)] * jnp.bfloat16(0.125)
        tail = query_tail(first, lens_ref, segs)
        folded = fold_heads(queries, tail, tail)
        low, tiles = key_bounds(first, used, lens_ref, segs)

        def score_step(at, width, place, top):
            scores = jnp.dot(kx_ref[pl.ds(at, width), :], folded, preferred_element_type=jnp.float32)
            score_ref[pl.ds(pl.multiple_of(place * TILE, TILE), width), :] = scores
            return jnp.maximum(top, jnp.max(row_eights(scores), axis=0))

        start = (
            jnp.zeros((8, 2 * TILE), jnp.float32),
            jnp.zeros((64, TILE), jnp.float32),
            jnp.zeros((64, TILE), jnp.float32),
        )

        def weigh(probs, at, state):
            total, one, two = state
            total = total + jnp.sum(row_eights(probs), axis=0)
            low_probs = probs.astype(jnp.bfloat16)
            one = one + jnp.dot(
                v_ref[0:64, pl.ds(at, TILE)], low_probs[:, 0:TILE], preferred_element_type=jnp.float32
            )
            two = two + jnp.dot(
                v_ref[64:128, pl.ds(at, TILE)], low_probs[:, TILE:], preferred_element_type=jnp.float32
            )
            return (total, one, two)

        def direct_step(at, width, place, state):
            scores = jnp.dot(kx_ref[pl.ds(at, width), :], folded, preferred_element_type=jnp.float32)
            for piece in range(0, width, TILE):
                state = weigh(jnp.exp(scores[piece : piece + TILE]), pl.multiple_of(at + piece, 128), state)
            return state

        def with_top():
            top = by_tiles((2, 1), low, tiles, score_step, jnp.full((8, 2 * TILE), -2.0 * BIG, jnp.float32))
            top = jnp.max(top, axis=0, keepdims=True)

            def value_step(at, width, place, state):
                scores = score_ref[pl.ds(pl.multiple_of(place * TILE, TILE), width), :]
                return weigh(jnp.exp(scores - top), at, state)

            return (top,) + by_tiles((1,), low, tiles, value_step, start)

        def without_top():
            return (jnp.zeros((1, 2 * TILE), jnp.float32),) + by_tiles((4, 2, 1), low, tiles, direct_step, start)

        top, total, one, two = lax.cond(small, without_top, with_top)
        total = jnp.sum(total, axis=0, keepdims=True)
        inverse = 1.0 / total
        att_ref[0:64, pl.ds(first, TILE)] = one * inverse[:, 0:TILE]
        att_ref[64:128, pl.ds(first, TILE)] = two * inverse[:, TILE:]
        lse = top + jnp.log(total)
        lse_ref[0:1, pl.ds(first, TILE)] = lse[:, 0:TILE]
        lse_ref[1:2, pl.ds(first, TILE)] = lse[:, TILE:]
        return carry

    lax.fori_loop(0, count, query_step, 0)


def attn_backward_kernel(
    segs, lens_ref, proj_ref, att_ref, lse_ref, gatt_ref, out_ref, kx_ref, vx_ref, k_ref, sums_ref
):
    used = used_of(lens_ref, segs)
    count = (used + TILE - 1) // TILE
    fill_keys(kx_ref, proj_ref, 128, lens_ref, segs, "segments")
    fill_keys(vx_ref, proj_ref, 256, lens_ref, segs, "ones")
    copy_padded(k_ref, proj_ref, 128)
    out_ref[...] = jnp.zeros_like(out_ref)
    sums_ref[...] = jnp.zeros_like(sums_ref)

    def query_step(index, carry):
        first = pl.multiple_of(index * TILE, TILE)
        queries = proj_ref[0:128, pl.ds(first, TILE)] * jnp.bfloat16(0.125)
        tail = query_tail(first, lens_ref, segs)
        lse_one = three_rows(-lse_ref[0:1, pl.ds(first, TILE)])
        lse_two = three_rows(-lse_ref[1:2, pl.ds(first, TILE)])
        folded = fold_heads(
            queries, jnp.concatenate([tail, lse_one], axis=0), jnp.concatenate([tail, lse_two], axis=0)
        )
        grads = gatt_ref[:, pl.ds(first, TILE)]
        weighted = grads.astype(jnp.float32) * att_ref[:, pl.ds(first, TILE)]
        delta_one = three_rows(-jnp.sum(weighted[0:64], axis=0, keepdims=True))
        delta_two = three_rows(-jnp.sum(weighted[64:128], axis=0, keepdims=True))
        grad_folded = fold_heads(grads, delta_one, delta_two)
        low, tiles = key_bounds(first, used, lens_ref, segs)
        transposed = (((1,), (1,)), ((), ()))

        def key_step(at, width, place, state):
            one, two = state

            def spot(piece):
                return pl.ds(pl.multiple_of(at + piece, 128), TILE)

            scores = jnp.dot(kx_ref[pl.ds(at, width), :], folded, preferred_element_type=jnp.float32)
            pulled = jnp.dot(vx_ref[pl.ds(at, width), :], grad_folded, preferred_element_type=jnp.float32)
            for piece in range(0, width, TILE):
                probs = jnp.exp(scores[piece : piece + TILE])
                score_grads = (probs * pulled[piece : piece + TILE]).astype(jnp.bfloat16)
                low_probs = probs.astype(jnp.bfloat16)
                sums_ref[0:128, spot(piece)] += lax.dot_general(
                    folded[0:128], score_grads, transposed, preferred_element_type=jnp.float32
                )
                sums_ref[128:256, spot(piece)] += lax.dot_general(
                    grad_folded[0:128], low_probs, transposed, preferred_element_type=jnp.float32
                )
                one = one + jnp.dot(
                    k_ref[0:64, spot(piece)], score_grads[:, 0:TILE], preferred_element_type=jnp.float32
                )
                two = two + jnp.dot(
                    k_ref[64:128, spot(piece)], score_grads[:, TILE:], preferred_element_type=jnp.float32
                )
            return (one, two)

        blank = jnp.zeros((64, TILE), jnp.float32)
        one, two = by_tiles((4, 2, 1), low, tiles, key_step, (blank, blank))
        out_ref[0:64, pl.ds(first, TILE)] = (one * 0.125).astype(jnp.bfloat16)
        out_ref[64:128, pl.ds(first, TILE)] = (two * 0.125).astype(jnp.bfloat16)
        return carry

    lax.fori_loop(0, count, query_step, 0)

    def write_step(index, carry):
        at = pl.multiple_of(index * TILE, TILE)
        out_ref[128:384, pl.ds(at, TILE)] = sums_ref[:, pl.ds(at, TILE)].astype(jnp.bfloat16)
        return carry

    lax.fori_loop(0, count, write_step, 0)


VMEM_LIMIT = 62 * 1024 * 1024
WHOLE = pl.BlockSpec(memory_space=pltpu.VMEM)
SCALARS = pl.BlockSpec(memory_space=pltpu.SMEM)
ANYWHERE = pl.BlockSpec(memory_space=pl.ANY)
PARAMS = pltpu.CompilerParams(vmem_limit_bytes=VMEM_LIMIT)


def attention_forward(projected, lengths_row):
    frames = projected.shape[1]
    segs = lengths_row.shape[0]
    return pl.pallas_call(
        functools.partial(attn_forward_kernel, segs),
        name="attention_forward",
        out_shape=(
            jax.ShapeDtypeStruct((128, frames), jnp.float32),
            jax.ShapeDtypeStruct((8, frames), jnp.float32),
        ),
        in_specs=[SCALARS, WHOLE],
        out_specs=(WHOLE, WHOLE),
        scratch_shapes=[
            pltpu.VMEM((frames + TILE, 256), jnp.bfloat16),
            pltpu.VMEM((128, frames + TILE), jnp.bfloat16),
            pltpu.VMEM((frames + TILE, 2 * TILE), jnp.float32),
        ],
        compiler_params=PARAMS,
    )(lengths_row, projected)


def attention_backward(projected, attended, log_sums, grad_attended, lengths_row):
    frames = projected.shape[1]
    segs = lengths_row.shape[0]
    return pl.pallas_call(
        functools.partial(attn_backward_kernel, segs),
        name="attention_backward",
        out_shape=jax.ShapeDtypeStruct((384, frames), jnp.bfloat16),
        in_specs=[SCALARS, WHOLE, WHOLE, WHOLE, WHOLE],
        out_specs=WHOLE,
        scratch_shapes=[
            pltpu.VMEM((frames + TILE, 256), jnp.bfloat16),
            pltpu.VMEM((frames + TILE, 256), jnp.bfloat16),
            pltpu.VMEM((128, frames + TILE), jnp.bfloat16),
            pltpu.VMEM((256, frames + TILE), jnp.float32),
        ],
        compiler_params=PARAMS,
        cost_estimate=pl.CostEstimate(flops=40_000_000_000, bytes_accessed=10_000_000, transcendentals=0),
    )(lengths_row, projected, attended, log_sums, grad_attended)


NT = (((1,), (1,)), ((), ()))


def dot(left, right):
    return jnp.dot(left, right, preferred_element_type=jnp.float32)


def dot_nt(left, right):
    return lax.dot_general(left, right, NT, preferred_element_type=jnp.float32)


def places_of(first, width):
    return lax.broadcasted_iota(jnp.int32, (1, width), 1) + first


def frame_masks(places, lens_ref, segs):
    used = used_of(lens_ref, segs)
    here = segment_of(places, lens_ref, segs)
    before = segment_of(places - 1, lens_ref, segs)
    after = segment_of(places + 1, lens_ref, segs)
    valid = places < used
    prev = valid & (here == before) & (places > 0)
    succ = valid & (here == after)
    return (valid.astype(jnp.float32), prev.astype(jnp.float32), succ.astype(jnp.float32))


def plane_of(utts, times):
    rest = utts // 2
    far = 4 if rest % 4 == 0 else 1
    near = rest // far
    return (near, far, near * times * 2)


def block_lanes(index, width):
    return pl.ds(pl.multiple_of(index * width, width), width)


def vector_row(ref):
    return ref[...].astype(jnp.float32).reshape(1, -1)


def vector_columns(refs, cols_ref):
    rows = [vector_row(ref) for ref in refs]
    rows.append(jnp.zeros((cols_ref.shape[1] - len(rows), rows[0].shape[1]), jnp.float32))
    cols_ref[...] = jnp.concatenate(rows, axis=0).T


def lane_fold(values):
    out = values[:, 0:128]
    for at in range(128, values.shape[1], 128):
        out = out + values[:, at : at + 128]
    return out


def column_sums(partial_ref):
    return jnp.sum(partial_ref[...].T, axis=0, keepdims=True)


def norm_frames(values):
    mean = jnp.mean(values, axis=0, keepdims=True)
    centered = values - mean
    spread = jnp.mean(centered * centered, axis=0, keepdims=True)
    scale = lax.rsqrt(spread + EPSILON)
    return (centered * scale, scale)


def norm_frames_back(grad_hat, hat, scale):
    mean_one = jnp.mean(grad_hat, axis=0, keepdims=True)
    mean_two = jnp.mean(grad_hat * hat, axis=0, keepdims=True)
    return scale * (grad_hat - mean_one - hat * mean_two)


BLOCK = 512
RES_BLOCK = 1024
PI = 3.141592653589793


def fit_even(function, terms):
    points = 0.25 * (1.0 - np.cos(np.pi * (np.arange(400) + 0.5) / 400))
    roots = np.sqrt(points)
    basis = np.polynomial.chebyshev.chebvander(8.0 * points - 1.0, terms - 1)
    fitted = np.linalg.lstsq(basis, function(roots), rcond=None)[0]
    series = np.polynomial.chebyshev.Chebyshev(fitted, domain=[0.0, 0.25])
    return [float(item) for item in series.convert(kind=np.polynomial.Polynomial).coef]


SIN_OVER = fit_even(lambda f: np.sin(PI * f) / f, 5)
ROUNDER = 1.5 * 2.0**23


def horner(coefficients, values):
    out = coefficients[-1]
    for item in coefficients[-2::-1]:
        out = out * values + item
    return out


def ffn_kernel(segs, utts, times, lens_ref, *refs):
    near, far, group = plane_of(utts, times)
    chips = group // 2
    ffn_body(segs, lens_ref, refs[0:5], refs[5:8], *refs[8:18], *refs[18 + chips :])
    pack_ref = refs[18 + chips]
    spot = lax.axis_index("utt") // 2 % near * times + lax.axis_index("tm")
    rows = pack_ref.shape[0] // group
    for step in range(chips):
        other = (spot + step) % chips
        for core in range(2):
            at = pl.multiple_of((core * chips + other) * rows, 16)
            refs[18 + step][core * rows : core * rows + rows, :] = pack_ref[pl.ds(at, rows), :]


def chunk_moves(utts, times, step):
    near, far, group = plane_of(utts, times)
    chips = group // 2
    moves = []
    for z in range(far):
        for core in range(2):
            for spot in range(chips):
                ends = []
                for place in (spot, (spot + step) % chips):
                    ends.append((((z * near + place // times) * 2 + core) * times) + place % times)
                moves.append(tuple(ends))
    return moves


def ffn_body(
    segs,
    lens_ref,
    vecs,
    wides,
    resid_hbm,
    att_hbm,
    cot_ref,
    wo_ref,
    we_ref,
    wr_ref,
    wd_ref,
    down_hbm,
    gtwo_hbm,
    gatt_hbm,
    pack_ref,
    gwd_ref,
    gwr_ref,
    gwe_ref,
    gwo_ref,
    cols_ref,
    wide_cols_ref,
    wo_t,
    we_t,
    wr_t,
    wd_t,
    part_ref,
    wide_part_ref,
    odd_ref,
    snaked_ref,
    gexp_ref,
    expand_ref,
    pull_ref,
    resid_ref,
    att_ref,
    down_ref,
    gtwo_ref,
    gatt_ref,
    copy_sem,
):
    frames = resid_ref.shape[1]
    half = BLOCK // 2
    moved = (
        (resid_hbm, resid_ref, BLOCK), (att_hbm, att_ref, BLOCK), (down_ref, down_hbm, half),
        (gtwo_ref, gtwo_hbm, BLOCK), (gatt_ref, gatt_hbm, BLOCK),
    )

    def move(which, index):
        source, target, width = moved[which]
        lanes = block_lanes(index, width)
        return pltpu.make_async_copy(source.at[:, lanes], target.at[:, lanes], copy_sem.at[which, index])

    for index in range(frames // BLOCK):
        move(0, index).start()
        move(1, index).start()
    vector_columns(vecs, cols_ref)
    vector_columns(wides, wide_cols_ref)
    wide_cols_ref[:, 3:4] = wide_cols_ref[:, 1:2] * (1.0 / PI)
    wide_cols_ref[:, 2:3] = 1.0 / wide_cols_ref[:, 2:3]
    wide_cols_ref[:, 4:5] = 2.0 * wide_cols_ref[:, 1:2] * wide_cols_ref[:, 2:3]
    wo_t[...] = wo_ref[...].T
    we_t[...] = we_ref[...].T
    wr_t[...] = wr_ref[...].T
    for tap in range(3):
        wd_t[tap] = wd_ref[tap].T
    for ref in (gwd_ref, gwr_ref, gwe_ref, gwo_ref, part_ref, wide_part_ref, odd_ref):
        ref[...] = jnp.zeros_like(ref)
    row_at = lax.broadcasted_iota(jnp.int32, (256, 256), 0)
    lane_at = lax.broadcasted_iota(jnp.int32, (256, 256), 1)
    source = jnp.where(lane_at < 128, 2 * lane_at, 2 * lane_at - 255)
    gather = (row_at == source).astype(jnp.float32).astype(jnp.bfloat16)
    row_half = lax.broadcasted_iota(jnp.int32, (128, 256), 0)
    lane_half = lax.broadcasted_iota(jnp.int32, (128, 256), 1)
    put_even = (lane_half == 2 * row_half).astype(jnp.float32).astype(jnp.bfloat16)
    put_odd = (lane_half == 2 * row_half + 1).astype(jnp.float32).astype(jnp.bfloat16)

    def column(index):
        return cols_ref[:, index : index + 1]

    def block_step(index, carry):
        first = pl.multiple_of(index * BLOCK, BLOCK)
        first_half = pl.multiple_of(index * half, half)
        valid, _, _ = frame_masks(places_of(first, BLOCK), lens_ref, segs)
        even_places = 2 * places_of(first_half, half + 128)
        even_valid, even_prev, even_next = frame_masks(even_places, lens_ref, segs)
        cot_here = cot_ref[:, pl.ds(first_half, half)].astype(jnp.float32) * even_valid[:, 0:half]
        after_at = pl.multiple_of(jnp.minimum(first_half + half, frames // 2 - 128), 128)
        cot_after = cot_ref[:, pl.ds(after_at, 128)].astype(jnp.float32)
        g_down = cot_here.astype(jnp.bfloat16)
        with_prev = jnp.concatenate([cot_here, cot_after], axis=1) * even_prev
        from_next = pltpu.roll(with_prev, half + 127, 1)[:, 0:half].astype(jnp.bfloat16)
        to_next = (cot_here * even_next[:, 0:half]).astype(jnp.bfloat16)
        thirds = []
        for at in range(0, half, 128):
            spread_even = dot(g_down[:, at : at + 128], put_even).astype(jnp.bfloat16)
            spread_next = dot(to_next[:, at : at + 128], put_odd).astype(jnp.bfloat16)
            spread_prev = dot(from_next[:, at : at + 128], put_odd).astype(jnp.bfloat16)
            thirds.append(
                dot(wd_ref[1], spread_even) + dot(wd_ref[2], spread_next) + dot(wd_ref[0], spread_prev)
            )
        g_three = jnp.concatenate(thirds, axis=1) * valid
        g_reduce = g_three.astype(jnp.bfloat16)
        part_ref[0] += lane_fold(cot_here)
        part_ref[1] += lane_fold(g_reduce.astype(jnp.float32))
        move(0, index).wait()
        move(1, index).wait()
        att_low = att_ref[:, pl.ds(first, BLOCK)].astype(jnp.bfloat16)
        resid_two = resid_ref[:, pl.ds(first, BLOCK)] + dot(wo_t[...], att_low) + column(0)
        hat, scale = norm_frames(resid_two)
        normed = (hat * column(1) + column(2)).astype(jnp.bfloat16)
        expand_ref[...] = dot(we_t[...], normed)
        pull_ref[...] = dot(wr_ref[...], g_reduce)
        for row in range(0, wr_ref.shape[0], 32):
            span = slice(row, row + 32)
            values = expand_ref[span, :] + wide_cols_ref[span, 0:1]
            turns = values * wide_cols_ref[span, 3:4]
            turns = turns - ((turns + ROUNDER) - ROUNDER)
            sine = horner(SIN_OVER, turns * turns) * turns
            sine_two = sine * sine
            cosine_two = jnp.maximum(1.0 - sine_two, 1e-12)
            double = sine * (cosine_two * lax.rsqrt(cosine_two))
            snaked_ref[span, :] = (values + sine_two * wide_cols_ref[span, 2:3]).astype(jnp.bfloat16)
            pulled = pull_ref[span, :]
            slope = pulled * double
            grown = pulled + slope * wide_cols_ref[span, 4:5]
            gexp_ref[span, :] = grown.astype(jnp.bfloat16)
            wide_part_ref[0, span, :] += lane_fold(slope * values)
            wide_part_ref[1, span, :] += lane_fold(pulled * sine_two)
            wide_part_ref[2, span, :] += lane_fold(grown)
        gwr_ref[...] += dot_nt(snaked_ref[...], g_reduce)
        gwe_ref[...] += dot_nt(gexp_ref[...], normed)
        reduced = dot(wr_t[...], snaked_ref[...])
        g_normed = dot(we_ref[...], gexp_ref[...])
        down_in = ((resid_two + reduced + column(3)) * valid).astype(jnp.bfloat16)
        evens = []
        odds = []
        for at in range(0, BLOCK, 256):
            both = dot(down_in[:, at : at + 256], gather)
            evens.append(both[:, 0:128])
            odds.append(both[:, 128:256])
        even_low = jnp.concatenate(evens, axis=1).astype(jnp.bfloat16)
        odd = jnp.concatenate(odds, axis=1)
        led = jnp.concatenate([odd_ref[...], odd], axis=1)
        odd_ref[...] = odd[:, half - 128 : half]
        before = (pltpu.roll(led, 1, 1)[:, 128:] * even_prev[:, 0:half]).astype(jnp.bfloat16)
        after = (odd * even_next[:, 0:half]).astype(jnp.bfloat16)
        down_pre = dot(wd_t[0], before) + dot(wd_t[1], even_low) + dot(wd_t[2], after) + column(4)
        down_ref[:, pl.ds(first_half, half)] = (down_pre * even_valid[:, 0:half]).astype(jnp.bfloat16)
        gwd_ref[0] += dot_nt(before, g_down)
        gwd_ref[1] += dot_nt(even_low, g_down)
        gwd_ref[2] += dot_nt(after, g_down)
        part_ref[2] += lane_fold(g_normed * hat)
        part_ref[3] += lane_fold(g_normed)
        g_two = g_three + norm_frames_back(g_normed * column(1), hat, scale)
        gtwo_ref[:, pl.ds(first, BLOCK)] = g_two
        g_attn = g_two.astype(jnp.bfloat16)
        part_ref[4] += lane_fold(g_attn.astype(jnp.float32))
        gwo_ref[...] += dot_nt(att_low, g_attn)
        gatt_ref[:, pl.ds(first, BLOCK)] = dot(wo_ref[...], g_attn).astype(jnp.bfloat16)
        for which in range(2, 5):
            move(which, index).start()
        return carry

    lax.fori_loop(0, frames // BLOCK, block_step, 0)
    over_beta_row = 1.0 / vector_row(wides[2])
    wide_rows = (
        column_sums(wide_part_ref.at[2]),
        column_sums(wide_part_ref.at[0]) * (2.0 * over_beta_row),
        -column_sums(wide_part_ref.at[1]) * (over_beta_row * over_beta_row),
    )
    rows = [column_sums(part_ref.at[index]) for index in range(5)]
    rows.extend(row[:, at : at + 256] for row in wide_rows for at in range(0, 1024, 256))
    rows.append(jnp.zeros((15, 256), jnp.float32))
    for tap in range(3):
        pack_ref[256 * tap : 256 * tap + 256, :] = gwd_ref[tap].astype(jnp.bfloat16)
    pack_ref[768:1792, :] = gwr_ref[...].astype(jnp.bfloat16)
    pack_ref[1792:2816, :] = gwe_ref[...].astype(jnp.bfloat16)
    pack_ref[2816:2944, :] = gwo_ref[...].astype(jnp.bfloat16)
    pack_ref[2944:2976, :] = jnp.concatenate(rows, axis=0).astype(jnp.bfloat16)
    for which in range(2, 5):
        for index in range(frames // BLOCK):
            move(which, index).wait()
    if pack_ref.shape[0] > 2976:
        pack_ref[2976:, :] = jnp.zeros((pack_ref.shape[0] - 2976, 256), jnp.bfloat16)


def feed_forward(utts, times, pack_rows, lengths_row, vecs, wides, resid_one, attended, cot, wo, we, wr, wd):
    frames = resid_one.shape[1]
    chunks = plane_of(utts, times)[2] // 2
    f32 = jnp.float32
    bf16 = jnp.bfloat16
    return pl.pallas_call(
        functools.partial(ffn_kernel, lengths_row.shape[0], utts, times),
        name="feed_forward",
        out_shape=(
            jax.ShapeDtypeStruct((256, frames // 2), bf16),
            jax.ShapeDtypeStruct((256, frames), f32),
            jax.ShapeDtypeStruct((128, frames), bf16),
        )
        + (jax.ShapeDtypeStruct((pack_rows // chunks, 256), bf16),) * chunks,
        in_specs=[SCALARS] + [WHOLE] * 8 + [ANYWHERE] * 2 + [WHOLE] * 5,
        out_specs=(ANYWHERE,) * 3 + (WHOLE,) * chunks,
        scratch_shapes=[
            pltpu.VMEM((pack_rows, 256), bf16),
            pltpu.VMEM((3, 256, 256), f32),
            pltpu.VMEM((1024, 256), f32),
            pltpu.VMEM((1024, 256), f32),
            pltpu.VMEM((128, 256), f32),
            pltpu.VMEM((256, 8), f32),
            pltpu.VMEM((1024, 8), f32),
            pltpu.VMEM((256, 128), bf16),
            pltpu.VMEM((1024, 256), bf16),
            pltpu.VMEM((256, 1024), bf16),
            pltpu.VMEM((3, 256, 256), bf16),
            pltpu.VMEM((5, 256, 128), f32),
            pltpu.VMEM((3, 1024, 128), f32),
            pltpu.VMEM((256, 128), f32),
            pltpu.VMEM((1024, BLOCK), bf16),
            pltpu.VMEM((1024, BLOCK), bf16),
            pltpu.VMEM((1024, BLOCK), f32),
            pltpu.VMEM((1024, BLOCK), f32),
            pltpu.VMEM((256, frames), f32),
            pltpu.VMEM((128, frames), f32),
            pltpu.VMEM((256, frames // 2), bf16),
            pltpu.VMEM((256, frames), f32),
            pltpu.VMEM((128, frames), bf16),
            pltpu.SemaphoreType.DMA((5, frames // BLOCK)),
        ],
        compiler_params=PARAMS,
    )(lengths_row, *vecs, *wides, resid_one, attended, cot, wo, we, wr, wd)


def mish_parts(values):
    grown = jnp.exp(jnp.minimum(values, 20.0))
    top = grown * (grown + 2.0)
    inverse = 1.0 / (top + 2.0)
    return (grown, top * inverse, inverse)


def mish_value(values):
    return values * mish_parts(values)[1]


def mish_slope(values):
    grown, ratio, inverse = mish_parts(values)
    return ratio + values * (4.0 * grown * (grown + 1.0)) * (inverse * inverse)


def segment_rows(places, lens_ref, segs):
    segment = segment_of(places, lens_ref, segs)
    row = lax.broadcasted_iota(jnp.int32, (128, places.shape[1]), 0)
    return ((row == segment) & (row < segs)).astype(jnp.float32).astype(jnp.bfloat16)


def stack_parts(values):
    top, mid, last = split_three(values)
    return jnp.concatenate(
        [top.astype(jnp.float32), mid.astype(jnp.float32), last.astype(jnp.float32)], axis=0
    ).astype(jnp.bfloat16)


def unstack_parts(stacked):
    return stacked[0:8] + stacked[8:16] + stacked[16:24]


def segment_totals(rows, hot):
    return unstack_parts(dot_nt(stack_parts(rows), hot))


def segment_values(stat, hot):
    return unstack_parts(dot(stack_parts(stat), hot))


def two_parts(values):
    top = values.astype(jnp.bfloat16)
    return (top, (values - top.astype(jnp.float32)).astype(jnp.bfloat16))


def segment_counts(lens_ref, segs):
    lane = lax.broadcasted_iota(jnp.int32, (8, 128), 1)
    counts = jnp.ones((8, 128), jnp.float32)
    for index in range(segs):
        counts = jnp.where(lane == index, lens_ref[index].astype(jnp.float32), counts)
    return counts


def conv_rows(padded_ref, first, prev, succ):
    width = prev.shape[1]
    wide = padded_ref[:, pl.ds(first, width + 256)].astype(jnp.float32)
    before = pltpu.roll(wide, 1, 1)[:, 128 : 128 + width] * prev
    after = pltpu.roll(wide, width + 255, 1)[:, 128 : 128 + width] * succ
    here = padded_ref[:, pl.ds(pl.multiple_of(first + 128, 128), width)]
    return (before.astype(jnp.bfloat16), here, after.astype(jnp.bfloat16))


def clear_pads(padded_ref):
    rows, width = padded_ref.shape
    padded_ref[:, 0:128] = jnp.zeros((rows, 128), padded_ref.dtype)
    padded_ref[:, width - 128 : width] = jnp.zeros((rows, 128), padded_ref.dtype)


def group_slice(group):
    return slice(32 * group, 32 * group + 32)


def stats_start(stat_ref):
    stat_ref[...] = jnp.zeros_like(stat_ref)


def stats_block(values_of, hot, stat_ref):
    folded = jnp.concatenate(
        [jnp.sum(values_of(group), axis=0, keepdims=True) for group in range(GROUPS)], axis=0
    )
    here = dot_nt(jnp.ones((16, hot.shape[1]), jnp.bfloat16), hot)[0:8]
    mean_here = segment_totals(folded, hot) / jnp.maximum(here * 32.0, 1.0)
    spread = segment_values(mean_here, hot)
    squares = []
    for group in range(GROUPS):
        centered = values_of(group) - spread[group : group + 1]
        squares.append(jnp.sum(centered * centered, axis=0, keepdims=True))
    squares_here = segment_totals(jnp.concatenate(squares, axis=0), hot)
    count, mean, total = stat_ref[0], stat_ref[1], stat_ref[2]
    share = here / jnp.maximum(count + here, 1.0)
    change = mean_here - mean
    stat_ref[0] = count + here
    stat_ref[1] = mean + change * share
    stat_ref[2] = total + squares_here + change * change * (count * 32.0) * share


def stats_scale(stat_ref):
    return lax.rsqrt(stat_ref[2] / jnp.maximum(stat_ref[0] * 32.0, 1.0) + EPSILON)


def halves_down(rows):
    width = rows.shape[1] // 2
    return jnp.concatenate([rows[:, 0:width], rows[:, width:]], axis=0)


def time_low_of(time_ref):
    embedded = time_ref[...].astype(jnp.float32)
    rows = mish_value(embedded).astype(jnp.bfloat16).astype(jnp.float32)
    return jnp.concatenate([rows, jnp.zeros_like(rows)], axis=0)


MESH_ID = pl.DeviceIdType.MESH


class Places:
    def __init__(self, utts, times):
        self.near, self.far, self.group = plane_of(utts, times)
        self.times = times
        self.devices = utts * times
        self.u = lax.axis_index("utt")
        self.t = lax.axis_index("tm")
        self.core = self.u % 2
        self.x = self.u // 2 % self.near
        self.z = self.u // 2 // self.near
        self.member = (self.x * times + self.t) * 2 + self.core

    def plane_peer(self, step):
        other = (self.member + step) % self.group
        rest = other // 2
        return ((self.z * self.near + rest // self.times) * 2 + other % 2, rest % self.times)

    def partner(self):
        return (self.u + 1 - 2 * self.core, self.t)

    def core_peer(self, step):
        other = (self.member // 2 + step) % (self.group // 2)
        return ((self.z * self.near + other // self.times) * 2 + self.core, other % self.times)

    def line_peer(self, step):
        return (((self.z + step) % self.far * self.near + self.x) * 2 + self.core, self.t)

    def greet(self, everyone):
        barrier = pltpu.get_barrier_semaphore()
        if everyone and self.devices <= 64:
            here = self.u * self.times + self.t
            others = [(here + step) % self.devices for step in range(1, self.devices)]
            peers = [(other // self.times, other % self.times) for other in others]
        else:
            peers = [self.plane_peer(step) for step in range(1, self.group)]
            peers += [self.line_peer(step) for step in range(1, self.far)]
        for peer in peers:
            pl.semaphore_signal(barrier, inc=1, device_id=peer, device_id_type=MESH_ID)
        pl.semaphore_wait(barrier, len(peers))


def aligned_rows(at, count):
    return pl.ds(pl.multiple_of(at, 16), count)


class Sender:
    def __init__(self, send_sem, recv_sem):
        self.send_sem, self.recv_sem = send_sem, recv_sem
        self.slot = 0
        self.copies = []

    def send(self, source, target, peer):
        copy = pltpu.make_async_remote_copy(
            src_ref=source,
            dst_ref=target,
            send_sem=self.send_sem.at[self.slot],
            recv_sem=self.recv_sem.at[self.slot],
            device_id=peer,
            device_id_type=MESH_ID,
        )
        copy.start()
        self.slot += 1
        self.copies.append(copy)

    def settle(self):
        for copy in self.copies:
            copy.wait()
        self.copies = []


def copy_semaphores(count):
    return [pltpu.SemaphoreType.DMA((count,)), pltpu.SemaphoreType.DMA((count,))]


def sum_scratch(utts, times, rows):
    near, far, group = plane_of(utts, times)
    part = rows // group
    return [
        pltpu.VMEM((group - 1, part, 256), jnp.bfloat16),
        pltpu.VMEM((part, 256), jnp.bfloat16),
        pltpu.VMEM((far - 1, part // far, 256), jnp.bfloat16),
    ] + copy_semaphores(2 * (group - 1) + 2 * (far - 1))


def sum_stages(places, pack_ref, out_ref, recv_a, sum_a, recv_b, send_sem, recv_sem):
    part, piece = sum_a.shape[0], recv_b.shape[1]
    group, far = places.group, places.far
    base = places.member * part
    sender = Sender(send_sem, recv_sem)

    def in_plane():
        for step in range(1, group):
            other = (places.member + step) % group
            sender.send(pack_ref.at[aligned_rows(other * part, part)], recv_a.at[step - 1], places.plane_peer(step))

    def on_line():
        sender.settle()
        total = pack_ref[aligned_rows(base, part), :].astype(jnp.float32)
        for step in range(1, group):
            total = total + recv_a[step - 1].astype(jnp.float32)
        sum_a[...] = total.astype(jnp.bfloat16)
        for step in range(1, far):
            other = (places.z + step) % far
            sender.send(sum_a.at[aligned_rows(other * piece, piece)], recv_b.at[step - 1], places.line_peer(step))

    def line_back():
        sender.settle()
        total = sum_a[aligned_rows(places.z * piece, piece), :].astype(jnp.float32)
        for step in range(1, far):
            total = total + recv_b[step - 1].astype(jnp.float32)
        mine = aligned_rows(base + places.z * piece, piece)
        out_ref[mine, :] = total.astype(jnp.bfloat16)
        for step in range(1, far):
            sender.send(out_ref.at[mine], out_ref.at[mine], places.line_peer(step))

    def plane_back():
        sender.settle()
        mine = aligned_rows(base, part)
        for step in range(1, group):
            sender.send(out_ref.at[mine], out_ref.at[mine], places.plane_peer(step))

    return [in_plane, on_line, line_back, plane_back, sender.settle]


def direct_scratch(utts, times, rows):
    devices = utts * times
    return [pltpu.VMEM((devices - 1, rows // devices, 256), jnp.bfloat16)] + copy_semaphores(2 * (devices - 1))


def direct_sum_stages(places, pack_ref, out_ref, recv_a, send_sem, recv_sem):
    devices = recv_a.shape[0] + 1
    piece = pack_ref.shape[0] // devices
    times = places.times
    here = places.u * times + places.t
    sender = Sender(send_sem, recv_sem)

    def to_all():
        for step in range(1, devices):
            other = (here + step) % devices
            peer = (other // times, other % times)
            sender.send(pack_ref.at[aligned_rows(other * piece, piece)], recv_a.at[step - 1], peer)

    def back():
        sender.settle()
        mine = aligned_rows(here * piece, piece)
        total = pack_ref[mine, :].astype(jnp.float32)
        for step in range(1, devices):
            total = total + recv_a[step - 1].astype(jnp.float32)
        out_ref[mine, :] = total.astype(jnp.bfloat16)
        for step in range(1, devices):
            other = (here + step) % devices
            sender.send(out_ref.at[mine], out_ref.at[mine], (other // times, other % times))

    def nothing():
        pass

    return [to_all, back, nothing, nothing, sender.settle]


def late_scratch(utts, times, rows):
    return (direct_scratch if utts * times <= 64 else sum_scratch)(utts, times, rows)


def late_stages(places, *refs):
    return (direct_sum_stages if places.devices <= 64 else sum_stages)(places, *refs)


def large_scratch(utts, times, rows):
    near, far, group = plane_of(utts, times)
    chips = group // 2
    half = rows // 2
    part = half // chips
    return [
        pltpu.VMEM((half, 256), jnp.bfloat16),
        pltpu.VMEM((half, 256), jnp.bfloat16),
        pltpu.VMEM((chips - 1, part, 256), jnp.bfloat16),
        pltpu.VMEM((part, 256), jnp.bfloat16),
        pltpu.VMEM((far - 1, part // far, 256), jnp.bfloat16),
    ] + copy_semaphores(2 * (1 + chips - 1 + far - 1))


def large_sum_stages(places, pack_ref, out_ref, recv_a, sum_a, recv_b, sum_b, recv_c, send_sem, recv_sem):
    half, part, piece = sum_a.shape[0], sum_b.shape[0], recv_c.shape[1]
    chips, far, core = places.group // 2, places.far, places.core
    spot = places.member // 2
    base = core * half + spot * part
    sender = Sender(send_sem, recv_sem)

    def between_cores():
        sender.send(pack_ref.at[aligned_rows((1 - core) * half, half)], recv_a, places.partner())

    def in_plane():
        sender.settle()
        own = pack_ref[aligned_rows(core * half, half), :].astype(jnp.float32)
        sum_a[...] = (own + recv_a[...].astype(jnp.float32)).astype(jnp.bfloat16)
        for step in range(1, chips):
            other = (spot + step) % chips
            sender.send(sum_a.at[aligned_rows(other * part, part)], recv_b.at[step - 1], places.core_peer(step))

    def on_line():
        sender.settle()
        total = sum_a[aligned_rows(spot * part, part), :].astype(jnp.float32)
        for step in range(1, chips):
            total = total + recv_b[step - 1].astype(jnp.float32)
        sum_b[...] = total.astype(jnp.bfloat16)
        for step in range(1, far):
            other = (places.z + step) % far
            sender.send(sum_b.at[aligned_rows(other * piece, piece)], recv_c.at[step - 1], places.line_peer(step))

    def line_back():
        sender.settle()
        total = sum_b[aligned_rows(places.z * piece, piece), :].astype(jnp.float32)
        for step in range(1, far):
            total = total + recv_c[step - 1].astype(jnp.float32)
        mine = aligned_rows(base + places.z * piece, piece)
        out_ref[mine, :] = total.astype(jnp.bfloat16)
        for step in range(1, far):
            sender.send(out_ref.at[mine], out_ref.at[mine], places.line_peer(step))

    def plane_back():
        sender.settle()
        mine = aligned_rows(base, part)
        for step in range(1, chips):
            sender.send(out_ref.at[mine], out_ref.at[mine], places.core_peer(step))

    def cores_back():
        sender.settle()
        mine = aligned_rows(core * half, half)
        sender.send(out_ref.at[mine], out_ref.at[mine], places.partner())

    return [between_cores, in_plane, on_line, line_back, plane_back, cores_back, sender.settle]


def chunk_scratch(utts, times, rows):
    near, far, group = plane_of(utts, times)
    part = rows // group
    return [
        pltpu.VMEM((2 * part, 256), jnp.bfloat16),
        pltpu.VMEM((part, 256), jnp.bfloat16),
        pltpu.VMEM((part, 256), jnp.bfloat16),
        pltpu.VMEM((far - 1, part // far, 256), jnp.bfloat16),
    ] + copy_semaphores(1 + 2 * (far - 1) + group // 2 - 1 + 1)


def chunk_sum_stages(places, chunk_refs, out_ref, sum_chips, recv_a, sum_a, recv_b, send_sem, recv_sem):
    part, piece = sum_a.shape[0], recv_b.shape[1]
    chips, far, core = places.group // 2, places.far, places.core
    spot = places.member // 2
    base = (core * chips + spot) * part
    sender = Sender(send_sem, recv_sem)

    def between_cores():
        total = chunk_refs[0][...].astype(jnp.float32)
        for ref in chunk_refs[1:]:
            total = total + ref[...].astype(jnp.float32)
        sum_chips[...] = total.astype(jnp.bfloat16)
        sender.send(sum_chips.at[aligned_rows((1 - core) * part, part)], recv_a, places.partner())

    def on_line():
        sender.settle()
        own = sum_chips[aligned_rows(core * part, part), :].astype(jnp.float32)
        sum_a[...] = (own + recv_a[...].astype(jnp.float32)).astype(jnp.bfloat16)
        for step in range(1, far):
            other = (places.z + step) % far
            sender.send(sum_a.at[aligned_rows(other * piece, piece)], recv_b.at[step - 1], places.line_peer(step))

    def line_back():
        sender.settle()
        total = sum_a[aligned_rows(places.z * piece, piece), :].astype(jnp.float32)
        for step in range(1, far):
            total = total + recv_b[step - 1].astype(jnp.float32)
        mine = aligned_rows(base + places.z * piece, piece)
        out_ref[mine, :] = total.astype(jnp.bfloat16)
        for step in range(1, far):
            sender.send(out_ref.at[mine], out_ref.at[mine], places.line_peer(step))

    def plane_back():
        sender.settle()
        mine = aligned_rows(base, part)
        for step in range(1, chips):
            sender.send(out_ref.at[mine], out_ref.at[mine], places.core_peer(step))

    def cores_back():
        sender.settle()
        mine = aligned_rows(core * chips * part, chips * part)
        sender.send(out_ref.at[mine], out_ref.at[mine], places.partner())

    return [between_cores, on_line, line_back, plane_back, cores_back, sender.settle]


def gather_stages(places, rows_of, own_ref, out_ref, own_sem, send_sem, recv_sem):
    chips, far = places.group // 2, places.far
    spot = places.member // 2
    sender = Sender(send_sem, recv_sem)
    local = []

    def on_line():
        mine = aligned_rows(((places.core * chips + spot) * far + places.z) * 16, 16)
        own_ref[...] = rows_of()
        copy = pltpu.make_async_copy(own_ref, out_ref.at[mine], own_sem.at[0])
        copy.start()
        local.append(copy)
        for step in range(1, far):
            sender.send(own_ref, out_ref.at[mine], places.line_peer(step))

    def in_plane():
        local[0].wait()
        sender.settle()
        mine = aligned_rows((places.core * chips + spot) * far * 16, far * 16)
        for step in range(1, chips):
            sender.send(out_ref.at[mine], out_ref.at[mine], places.core_peer(step))

    def between_cores():
        sender.settle()
        mine = aligned_rows(places.core * chips * far * 16, chips * far * 16)
        sender.send(out_ref.at[mine], out_ref.at[mine], places.partner())

    return [on_line, in_plane, between_cores, sender.settle]


def gather_scratch(utts, times, width):
    near, far, group = plane_of(utts, times)
    return [
        pltpu.VMEM((16, width), jnp.bfloat16),
        pltpu.SemaphoreType.DMA((1,)),
    ] + copy_semaphores(group // 2 - 1 + far - 1 + 1)


def res_forward_kernel(
    segs,
    utts,
    times,
    lens_ref,
    *refs,
):
    vecs = refs[0:10]
    res_forward_body(segs, utts, times, lens_ref, vecs, *refs[10:])


def res_forward_body(
    segs,
    utts,
    times,
    lens_ref,
    vecs,
    noisy_ref,
    mean_ref,
    time_ref,
    wc1_ref,
    tw_ref,
    wc2_ref,
    wsk_ref,
    wh_ref,
    hat_one_hbm,
    act_hbm,
    hat_two_hbm,
    hat_norm_hbm,
    scale_norm_ref,
    resid_hbm,
    proj_hbm,
    scales_ref,
    xin_hbm,
    time_all_ref,
    cols_ref,
    wc1_t,
    wc2_t,
    wsk_t,
    wh_t,
    pre_ref,
    stat_ref,
    time_cols_ref,
    mean_all_ref,
    hat_one_ref,
    act_ref,
    hat_two_ref,
    hat_norm_ref,
    resid_ref,
    proj_ref,
    xin_ref,
    store_sem,
    send_mean,
    arrive_mean,
    *gather_refs,
):
    frames = noisy_ref.shape[1]
    blocks = frames // RES_BLOCK
    stores = (
        (hat_one_ref, hat_one_hbm), (act_ref.at[:, 128 : 128 + frames], act_hbm), (hat_two_ref, hat_two_hbm),
        (hat_norm_ref, hat_norm_hbm), (resid_ref, resid_hbm), (proj_ref, proj_hbm),
        (xin_ref.at[:, 128 : 128 + frames], xin_hbm),
    )

    def store(which, index):
        source, target = stores[which]
        lanes = block_lanes(index, RES_BLOCK)
        return pltpu.make_async_copy(source.at[:, lanes], target.at[:, lanes], store_sem.at[which, index])

    spots = Places(utts, times)
    embedded = gather_stages(
        spots, lambda: halves_down(time_low_of(time_ref)[0:8]).astype(jnp.bfloat16),
        gather_refs[0], time_all_ref, *gather_refs[1:4]
    )
    means = Sender(send_mean, arrive_mean)
    width = frames // times
    spots.greet(False)
    own_lanes = pl.ds(pl.multiple_of(spots.t * width, 128), width)
    for step in range(1, times):
        means.send(mean_ref, mean_all_ref.at[:, own_lanes], (spots.u, (spots.t + step) % times))
    mean_all_ref[:, own_lanes] = mean_ref[...]
    embedded[0]()
    vector_columns(vecs, cols_ref)
    for tap in range(3):
        columns = wc1_ref[tap].astype(jnp.float32).T.astype(jnp.bfloat16)
        wc1_t[0, :, 80 * tap : 80 * tap + 80] = columns[:, 0:80]
        wc1_t[1, :, 80 * tap : 80 * tap + 80] = columns[:, 80:160]
        wc2_t[:, 256 * tap : 256 * tap + 256] = wc2_ref[tap].T
    wsk_t[...] = wsk_ref[...].astype(jnp.float32).T.astype(jnp.bfloat16)
    wh_t[...] = wh_ref[...].T
    time_rows = dot(time_low_of(time_ref).astype(jnp.bfloat16), tw_ref[...]) + vector_row(vecs[3])
    seg_row = lax.broadcasted_iota(jnp.int32, (16, 256), 0)
    time_rows = jnp.where(seg_row < segs, time_rows, 0.0)
    time_cols = jnp.concatenate([time_rows, jnp.zeros((112, 256), jnp.float32)], axis=0).T
    time_top, time_mid = two_parts(time_cols)
    time_cols_ref[:, 0:128] = time_top
    time_cols_ref[:, 128:256] = time_mid
    clear_pads(xin_ref)
    clear_pads(act_ref)

    def column(index):
        return cols_ref[:, index : index + 1]

    def input_phase(source_ref, row):
        def step(index, carry):
            first = pl.multiple_of(index * RES_BLOCK, RES_BLOCK)
            valid, _, _ = frame_masks(places_of(first, RES_BLOCK), lens_ref, segs)
            rows = source_ref[:, pl.ds(first, RES_BLOCK)].astype(jnp.float32) * valid
            here = pl.ds(pl.multiple_of(first + 128, 128), RES_BLOCK)
            xin_ref[row : row + 80, here] = rows.astype(jnp.bfloat16)
            return carry

        lax.fori_loop(0, blocks, step, 0)

    def taps_of(padded_ref, index):
        first = pl.multiple_of(index * RES_BLOCK, RES_BLOCK)
        places = places_of(first, RES_BLOCK)
        _, prev, succ = frame_masks(places, lens_ref, segs)
        return (first, places, jnp.concatenate(conv_rows(padded_ref, first, prev, succ), axis=0))

    def conv_phase(padded_ref, weight, start_of):
        stats_start(stat_ref)

        def step(index, carry):
            first, places, taps = taps_of(padded_ref, index)
            pre_ref[:, pl.ds(first, RES_BLOCK)] = dot(weight[...], taps) + start_of(first)
            stats_block(
                lambda group: pre_ref[group_slice(group), pl.ds(first, RES_BLOCK)],
                segment_rows(places, lens_ref, segs),
                stat_ref,
            )
            return carry

        lax.fori_loop(0, blocks, step, 0)

    def noisy_step(index, carry):
        first, _, taps = taps_of(xin_ref.at[0:80], index)
        pre_ref[:, pl.ds(first, RES_BLOCK)] = dot(wc1_t[0], taps) + column(0)
        return carry

    input_phase(noisy_ref, 0)
    lax.fori_loop(0, blocks, noisy_step, 0)
    means.settle()
    embedded[1]()
    input_phase(mean_all_ref, 80)
    conv_phase(xin_ref.at[80:160], wc1_t.at[1], lambda first: pre_ref[:, pl.ds(first, RES_BLOCK)])
    for index in range(blocks):
        store(6, index).start()
    embedded[2]()
    scales_ref[0] = stats_scale(stat_ref)

    def act_step(index, carry):
        first = pl.multiple_of(index * RES_BLOCK, RES_BLOCK)
        places = places_of(first, RES_BLOCK)
        valid, _, _ = frame_masks(places, lens_ref, segs)
        hot = segment_rows(places, lens_ref, segs)
        mean = segment_values(stat_ref[1], hot)
        scale = segment_values(scales_ref[0], hot)
        timed = dot(time_cols_ref[...], jnp.concatenate([hot, hot], axis=0))
        for group in range(GROUPS):
            rows = group_slice(group)
            hat = (pre_ref[rows, pl.ds(first, RES_BLOCK)] - mean[group : group + 1]) * scale[group : group + 1]
            hat_one_ref[rows, pl.ds(first, RES_BLOCK)] = hat.astype(jnp.bfloat16)
            value = mish_value(hat * cols_ref[rows, 1:2] + cols_ref[rows, 2:3]) + timed[rows]
            act_ref[rows, pl.ds(pl.multiple_of(first + 128, 128), RES_BLOCK)] = (value * valid).astype(jnp.bfloat16)
        store(0, index).start()
        store(1, index).start()
        return carry

    lax.fori_loop(0, blocks, act_step, 0)
    conv_phase(act_ref, wc2_t, lambda first: column(4))
    embedded[3]()
    scales_ref[1] = stats_scale(stat_ref)

    def resid_step(index, carry):
        first = pl.multiple_of(index * RES_BLOCK, RES_BLOCK)
        places = places_of(first, RES_BLOCK)
        valid, _, _ = frame_masks(places, lens_ref, segs)
        hot = segment_rows(places, lens_ref, segs)
        mean = segment_values(stat_ref[1], hot)
        scale = segment_values(scales_ref[1], hot)
        skip = dot(wsk_t[...], xin_ref[:, pl.ds(pl.multiple_of(first + 128, 128), RES_BLOCK)])
        for group in range(GROUPS):
            rows = group_slice(group)
            hat = (pre_ref[rows, pl.ds(first, RES_BLOCK)] - mean[group : group + 1]) * scale[group : group + 1]
            hat_two_ref[rows, pl.ds(first, RES_BLOCK)] = hat.astype(jnp.bfloat16)
            value = mish_value(hat * cols_ref[rows, 5:6] + cols_ref[rows, 6:7]) * valid
            resid_ref[rows, pl.ds(first, RES_BLOCK)] = value + skip[rows] + cols_ref[rows, 7:8]
        hat, scale = norm_frames(resid_ref[:, pl.ds(first, RES_BLOCK)])
        hat_norm_ref[:, pl.ds(first, RES_BLOCK)] = hat.astype(jnp.bfloat16)
        scale_norm_ref[:, pl.ds(first, RES_BLOCK)] = jnp.broadcast_to(scale, (8, RES_BLOCK))
        normed = (hat * column(8) + column(9)).astype(jnp.bfloat16)
        proj_ref[:, pl.ds(first, RES_BLOCK)] = dot(wh_t[...], normed).astype(jnp.bfloat16)
        for which in range(2, 6):
            store(which, index).start()
        return carry

    lax.fori_loop(0, blocks, resid_step, 0)
    for which in range(7):
        for index in range(blocks):
            store(which, index).wait()


def res_forward(utts, times, lengths_row, vecs, noisy, mean, embedded, wc1, tw, wc2, wsk, wh):
    frames = noisy.shape[1]
    f32 = jnp.float32
    bf16 = jnp.bfloat16
    return pl.pallas_call(
        functools.partial(res_forward_kernel, lengths_row.shape[0], utts, times),
        name="res_forward",
        out_shape=(
            jax.ShapeDtypeStruct((256, frames), bf16),
            jax.ShapeDtypeStruct((256, frames), bf16),
            jax.ShapeDtypeStruct((256, frames), bf16),
            jax.ShapeDtypeStruct((256, frames), bf16),
            jax.ShapeDtypeStruct((8, frames), f32),
            jax.ShapeDtypeStruct((256, frames), f32),
            jax.ShapeDtypeStruct((384, frames), bf16),
            jax.ShapeDtypeStruct((2, 8, 128), f32),
            jax.ShapeDtypeStruct((160, frames), bf16),
            jax.ShapeDtypeStruct((utts * times * 16, embedded.shape[1] // 2), bf16),
        ),
        in_specs=[SCALARS] + [WHOLE] * 18,
        out_specs=(ANYWHERE,) * 4 + (WHOLE,) + (ANYWHERE,) * 2 + (WHOLE,) + (ANYWHERE,) * 2,
        scratch_shapes=[
            pltpu.VMEM((256, 16), f32),
            pltpu.VMEM((2, 256, 240), bf16),
            pltpu.VMEM((256, 768), bf16),
            pltpu.VMEM((256, 160), bf16),
            pltpu.VMEM((384, 256), bf16),
            pltpu.VMEM((256, frames), f32),
            pltpu.VMEM((3, 8, 128), f32),
            pltpu.VMEM((256, 256), bf16),
            pltpu.VMEM((80, frames), bf16),
            pltpu.VMEM((256, frames), bf16),
            pltpu.VMEM((256, frames + 256), bf16),
            pltpu.VMEM((256, frames), bf16),
            pltpu.VMEM((256, frames), bf16),
            pltpu.VMEM((256, frames), f32),
            pltpu.VMEM((384, frames), bf16),
            pltpu.VMEM((160, frames + 256), bf16),
            pltpu.SemaphoreType.DMA((7, frames // RES_BLOCK)),
        ]
        + copy_semaphores(times - 1)
        + gather_scratch(utts, times, embedded.shape[1] // 2),
        compiler_params=pltpu.CompilerParams(
            vmem_limit_bytes=VMEM_LIMIT, collective_id=0, has_side_effects=True
        ),
    )(lengths_row, *vecs, noisy, mean, embedded, wc1, tw, wc2, wsk, wh)


def norm_back_sums(grad_of, hat_ref, gain_index, shift_index, first, hot, cols_ref, dhat_ref, part_ref, part_at, stat_ref):
    ones = []
    twos = []
    for group in range(GROUPS):
        rows = group_slice(group)
        hat = hat_ref[rows, pl.ds(first, RES_BLOCK)].astype(jnp.float32)
        gain = cols_ref[rows, gain_index : gain_index + 1]
        slope = mish_slope(hat * gain + cols_ref[rows, shift_index : shift_index + 1])
        grad = grad_of(rows) * slope
        part_ref[part_at, rows, :] += lane_fold(grad * hat)
        part_ref[part_at + 1, rows, :] += lane_fold(grad)
        grad_hat = grad * gain
        dhat_ref[rows, pl.ds(first, RES_BLOCK)] = grad_hat
        ones.append(jnp.sum(grad_hat, axis=0, keepdims=True))
        twos.append(jnp.sum(grad_hat * hat, axis=0, keepdims=True))
    stat_ref[0] += segment_totals(jnp.concatenate(ones, axis=0), hot)
    stat_ref[1] += segment_totals(jnp.concatenate(twos, axis=0), hot)


def norm_back_apply(hat_ref, scale_stat, first, hot, counts, dhat_ref, stat_ref, padded_ref, part_ref, part_at):
    mean_one = segment_values(stat_ref[0] / (counts * 32.0), hot)
    mean_two = segment_values(stat_ref[1] / (counts * 32.0), hot)
    scale = segment_values(scale_stat, hot)
    for group in range(GROUPS):
        rows = group_slice(group)
        at = slice(group, group + 1)
        hat = hat_ref[rows, pl.ds(first, RES_BLOCK)].astype(jnp.float32)
        grad = scale[at] * (dhat_ref[rows, pl.ds(first, RES_BLOCK)] - mean_one[at] - hat * mean_two[at])
        part_ref[part_at, rows, :] += lane_fold(grad)
        padded_ref[rows, pl.ds(pl.multiple_of(first + 128, 128), RES_BLOCK)] = grad.astype(jnp.bfloat16)


def res_backward_kernel(segs, utts, times, lens_ref, *refs):
    chunks = 10 + plane_of(utts, times)[2] // 2
    res_backward_body(segs, utts, times, lens_ref, refs[0:10], refs[10:chunks], *refs[chunks:])


def res_backward_body(
    segs,
    utts,
    times,
    lens_ref,
    vecs,
    tail_refs,
    gtwo_hbm,
    gproj_hbm,
    hat_norm_hbm,
    scale_norm_ref,
    hat_two_hbm,
    act_hbm,
    hat_one_hbm,
    scales_ref,
    xin_hbm,
    time_ref,
    wc1_ref,
    tw_ref,
    wc2_ref,
    wsk_ref,
    wh_ref,
    gnoisy_hbm,
    gmean_out_ref,
    gtime_ref,
    early_out,
    middle_out,
    late_out,
    tail_out,
    gseg_all_ref,
    cols_ref,
    wc1_b,
    wc2_b,
    gsk_ref,
    dhat_ref,
    gpre_ref,
    part_ref,
    stat_ref,
    gwh_ref,
    gwsk_ref,
    gwc2_ref,
    gwc1_ref,
    gseg_ref,
    gtwo_ref,
    gproj_ref,
    hat_norm_ref,
    hat_two_ref,
    act_ref,
    hat_one_ref,
    xin_ref,
    gnoisy_ref,
    load_sem,
    store_sem,
    gmean_ref,
    recv_mean,
    early_ref,
    middle_ref,
    late_ref,
    *stream_refs,
):
    frames = gtwo_ref.shape[1]
    blocks = frames // RES_BLOCK
    blocked = (
        (gproj_hbm, gproj_ref), (hat_norm_hbm, hat_norm_ref), (gtwo_hbm, gtwo_ref), (hat_two_hbm, hat_two_ref),
        (xin_hbm, xin_ref), (act_hbm, act_ref), (hat_one_hbm, hat_one_ref),
    )

    def load(which, index):
        source, target = blocked[which]
        lanes = block_lanes(index, RES_BLOCK)
        return pltpu.make_async_copy(source.at[:, lanes], target.at[:, lanes], load_sem.at[which, index])

    def store(index):
        lanes = block_lanes(index, BLOCK)
        return pltpu.make_async_copy(gnoisy_ref.at[:, lanes], gnoisy_hbm.at[:, lanes], store_sem.at[index])

    for index in range(blocks):
        for which in range(5):
            load(which, index).start()
    for which in range(5, 7):
        for index in range(blocks):
            load(which, index).start()
    spots = Places(utts, times)
    late_end = 10 + len(late_scratch(utts, times, late_ref.shape[0]))
    rest_refs = stream_refs[late_end:]
    early = sum_stages(spots, early_ref, early_out, *stream_refs[0:5])
    middle = sum_stages(spots, middle_ref, middle_out, *stream_refs[5:10])
    late = late_stages(spots, late_ref, late_out, *stream_refs[10:late_end])
    segments = gather_stages(
        spots, lambda: halves_down(gseg_ref[...].T[0:8]).astype(jnp.bfloat16),
        rest_refs[0], gseg_all_ref, *rest_refs[1:4]
    )
    means = Sender(*rest_refs[4:6])
    tail = chunk_sum_stages(spots, tail_refs, tail_out, *rest_refs[6:12])
    spots.greet(True)
    tail[0]()
    vector_columns(vecs, cols_ref)
    for tap in range(3):
        wc1_b[:, 256 * tap : 256 * tap + 256] = wc1_ref[tap]
        wc2_b[:, 256 * tap : 256 * tap + 256] = wc2_ref[tap]
    for ref in (part_ref, stat_ref, gwh_ref, gwsk_ref, gwc2_ref, gwc1_ref, gseg_ref):
        ref[...] = jnp.zeros_like(ref)
    clear_pads(gpre_ref)
    counts = segment_counts(lens_ref, segs)

    def column(index):
        return cols_ref[:, index : index + 1]

    def layout(index):
        first = pl.multiple_of(index * RES_BLOCK, RES_BLOCK)
        places = places_of(first, RES_BLOCK)
        return (first, places, frame_masks(places, lens_ref, segs))

    def project_step(index, carry):
        for which in range(5):
            load(which, index).wait()
        first, places, (valid, _, _) = layout(index)
        hot = segment_rows(places, lens_ref, segs)
        gproj = gproj_ref[:, pl.ds(first, RES_BLOCK)]
        g_normed = dot(wh_ref[...], gproj)
        hat = hat_norm_ref[:, pl.ds(first, RES_BLOCK)].astype(jnp.float32)
        normed = (hat * column(8) + column(9)).astype(jnp.bfloat16)
        gwh_ref[...] += dot_nt(gproj, normed)
        part_ref[0] += lane_fold(g_normed * hat)
        part_ref[1] += lane_fold(g_normed)
        back = norm_frames_back(g_normed * column(8), hat, scale_norm_ref[0:1, pl.ds(first, RES_BLOCK)])
        dhat_ref[:, pl.ds(first, RES_BLOCK)] = gtwo_ref[:, pl.ds(first, RES_BLOCK)] + back
        g_skip = dhat_ref[:, pl.ds(first, RES_BLOCK)].astype(jnp.bfloat16)
        gsk_ref[:, pl.ds(first, RES_BLOCK)] = g_skip
        part_ref[2] += lane_fold(g_skip.astype(jnp.float32))
        gwsk_ref[...] += dot_nt(xin_ref[:, pl.ds(first, RES_BLOCK)], g_skip)
        norm_back_sums(
            lambda rows: dhat_ref[rows, pl.ds(first, RES_BLOCK)] * valid,
            hat_two_ref, 5, 6, first, hot, cols_ref, dhat_ref, part_ref, 3, stat_ref,
        )
        return carry

    lax.fori_loop(0, blocks, project_step, 0)
    tail[1]()
    early_ref[0:384, :] = gwh_ref[...].astype(jnp.bfloat16)
    early_ref[384:512, :] = gwsk_ref[0:128, :].astype(jnp.bfloat16)
    fill_rest(early_ref, 512)
    early[0]()

    def apply_two_step(index, carry):
        first, places, _ = layout(index)
        hot = segment_rows(places, lens_ref, segs)
        norm_back_apply(hat_two_ref, scales_ref[1], first, hot, counts, dhat_ref, stat_ref, gpre_ref, part_ref, 5)
        return carry

    lax.fori_loop(0, blocks, apply_two_step, 0)
    stat_ref[...] = jnp.zeros_like(stat_ref)

    def conv_two_weight_step(index, carry):
        load(5, index).wait()
        load(6, index).wait()
        first, places, (valid, prev, succ) = layout(index)
        taps = jnp.concatenate(conv_rows(gpre_ref, first, prev, succ)[::-1], axis=0)
        gwc2_ref[...] += dot_nt(act_ref[:, pl.ds(first, RES_BLOCK)], taps)
        return carry

    lax.fori_loop(0, blocks, conv_two_weight_step, 0)
    for tap in range(3):
        middle_ref[256 * tap : 256 * tap + 256, :] = gwc2_ref[:, 256 * tap : 256 * tap + 256].astype(jnp.bfloat16)
    middle_ref[768:800, :] = gwsk_ref[128:160, :].astype(jnp.bfloat16)
    fill_rest(middle_ref, 800)
    middle[0]()
    tail[2]()
    early[1]()

    def conv_two_step(index, carry):
        first, places, (valid, prev, succ) = layout(index)
        hot = segment_rows(places, lens_ref, segs)
        before, here, after = conv_rows(gpre_ref, first, prev, succ)
        taps = jnp.concatenate([after, here, before], axis=0)
        dhat_ref[:, pl.ds(first, RES_BLOCK)] = dot(wc2_b[...], taps) * valid
        top, mid = two_parts(dhat_ref[:, pl.ds(first, RES_BLOCK)])
        gseg_ref[...] += dot_nt(top, hot) + dot_nt(mid, hot)
        norm_back_sums(
            lambda rows: dhat_ref[rows, pl.ds(first, RES_BLOCK)],
            hat_one_ref, 1, 2, first, hot, cols_ref, dhat_ref, part_ref, 6, stat_ref,
        )
        return carry

    lax.fori_loop(0, blocks // 2, conv_two_step, 0)
    tail[3]()
    lax.fori_loop(blocks // 2, blocks, conv_two_step, 0)
    segments[0]()
    middle[1]()
    early[2]()

    def apply_one_step(index, carry):
        first, places, _ = layout(index)
        hot = segment_rows(places, lens_ref, segs)
        norm_back_apply(hat_one_ref, scales_ref[0], first, hot, counts, dhat_ref, stat_ref, gpre_ref, part_ref, 8)
        return carry

    lax.fori_loop(0, blocks, apply_one_step, 0)
    segments[1]()
    early[3]()

    def conv_one_step(index, carry):
        first, places, (valid, prev, succ) = layout(index)
        before, here, after = conv_rows(gpre_ref, first, prev, succ)
        taps = jnp.concatenate([after, here, before], axis=0)
        gwc1_ref[...] += dot_nt(xin_ref[:, pl.ds(first, RES_BLOCK)], taps)
        return carry

    lax.fori_loop(0, blocks, conv_one_step, 0)
    for tap in range(3):
        late_ref[160 * tap : 160 * tap + 160, :] = gwc1_ref[:, 256 * tap : 256 * tap + 256].astype(jnp.bfloat16)
    rows = [column_sums(part_ref.at[index]) for index in range(9)]
    rows.append(jnp.zeros((7, 256), jnp.float32))
    late_ref[480:496, :] = jnp.concatenate(rows, axis=0).astype(jnp.bfloat16)
    fill_rest(late_ref, 496)
    late[0]()
    segments[2]()
    middle[2]()

    def inputs_step(index, carry):
        first = pl.multiple_of(index * BLOCK, BLOCK)
        valid, prev, succ = frame_masks(places_of(first, BLOCK), lens_ref, segs)
        taps = jnp.concatenate(conv_rows(gpre_ref, first, prev, succ)[::-1], axis=0)
        g_in = dot(wc1_b[...], taps) + dot(wsk_ref[...], gsk_ref[:, pl.ds(first, BLOCK)])
        g_in = g_in * valid
        gnoisy_ref[:, pl.ds(first, BLOCK)] = g_in[0:80]
        store(index).start()
        gmean_ref[:, pl.ds(first, BLOCK)] = g_in[80:160].astype(jnp.bfloat16)
        return carry

    small_blocks = frames // BLOCK
    width = frames // times
    for step in range(1, times + 1):
        owner = (spots.t + step) % times
        lax.fori_loop(owner * (small_blocks // times), (owner + 1) * (small_blocks // times), inputs_step, 0)
        if step < times:
            lanes = pl.ds(pl.multiple_of(owner * width, 128), width)
            means.send(gmean_ref.at[:, lanes], recv_mean.at[step - 1], (spots.u, owner))
    late[1]()
    middle[3]()
    tail[4]()
    segments[3]()
    early[4]()
    grad_low = dot_nt(gseg_ref[...].T[0:16].astype(jnp.bfloat16), tw_ref[...])
    gtime_ref[...] = grad_low[0:8] * mish_slope(time_ref[...].astype(jnp.float32))
    late[2]()
    means.settle()
    total = gmean_ref[:, pl.ds(pl.multiple_of(spots.t * width, 128), width)].astype(jnp.float32)
    for step in range(1, times):
        total = total + recv_mean[step - 1].astype(jnp.float32)
    gmean_out_ref[...] = total
    late[3]()
    middle[4]()
    tail[5]()
    late[4]()
    for index in range(small_blocks):
        store(index).wait()


def fill_rest(ref, rows):
    if ref.shape[0] > rows:
        ref[rows:, :] = jnp.zeros((ref.shape[0] - rows, ref.shape[1]), ref.dtype)


def padded_rows(rows, utts, times):
    return rows + -rows % (16 * utts * times)


def res_backward(
    utts, times, lengths_row, vecs, gtwo, gproj, hat_norm, scale_norm, hat_two, act, hat_one, scales, xin,
    embedded, wc1, tw, wc2, wsk, wh, tail,
):
    frames = gtwo.shape[1]
    f32 = jnp.float32
    bf16 = jnp.bfloat16
    early, middle, late = (padded_rows(rows, utts, times) for rows in (512, 800, 496))
    devices = utts * times
    tail_rows = tail[0].shape[0] * len(tail)
    return pl.pallas_call(
        functools.partial(res_backward_kernel, lengths_row.shape[0], utts, times),
        name="res_backward",
        out_shape=(
            jax.ShapeDtypeStruct((80, frames), f32),
            jax.ShapeDtypeStruct((80, frames // times), f32),
            jax.ShapeDtypeStruct(embedded.shape, f32),
            jax.ShapeDtypeStruct((early, 256), bf16),
            jax.ShapeDtypeStruct((middle, 256), bf16),
            jax.ShapeDtypeStruct((late, 256), bf16),
            jax.ShapeDtypeStruct((tail_rows, 256), bf16),
            jax.ShapeDtypeStruct((devices * 16, 128), bf16),
        ),
        in_specs=[SCALARS] + [WHOLE] * (10 + len(tail)) + [ANYWHERE] * 3 + [WHOLE] + [ANYWHERE] * 3 + [WHOLE] + [ANYWHERE] + [WHOLE] * 6,
        out_specs=(ANYWHERE,) + (WHOLE,) * 6 + (ANYWHERE,),
        scratch_shapes=[
            pltpu.VMEM((256, 16), f32),
            pltpu.VMEM((160, 768), bf16),
            pltpu.VMEM((256, 768), bf16),
            pltpu.VMEM((256, frames), bf16),
            pltpu.VMEM((256, frames), f32),
            pltpu.VMEM((256, frames + 256), bf16),
            pltpu.VMEM((9, 256, 128), f32),
            pltpu.VMEM((2, 8, 128), f32),
            pltpu.VMEM((384, 256), f32),
            pltpu.VMEM((160, 256), f32),
            pltpu.VMEM((256, 768), f32),
            pltpu.VMEM((160, 768), f32),
            pltpu.VMEM((256, 128), f32),
            pltpu.VMEM((256, frames), f32),
            pltpu.VMEM((384, frames), bf16),
            pltpu.VMEM((256, frames), bf16),
            pltpu.VMEM((256, frames), bf16),
            pltpu.VMEM((256, frames), bf16),
            pltpu.VMEM((256, frames), bf16),
            pltpu.VMEM((160, frames), bf16),
            pltpu.VMEM((80, frames), f32),
            pltpu.SemaphoreType.DMA((7, frames // RES_BLOCK)),
            pltpu.SemaphoreType.DMA((frames // BLOCK,)),
            pltpu.VMEM((80, frames), bf16),
            pltpu.VMEM((times - 1, 80, frames // times), bf16),
            pltpu.VMEM((early, 256), bf16),
            pltpu.VMEM((middle, 256), bf16),
            pltpu.VMEM((late, 256), bf16),
        ]
        + sum_scratch(utts, times, early)
        + sum_scratch(utts, times, middle)
        + late_scratch(utts, times, late)
        + gather_scratch(utts, times, 128)
        + copy_semaphores(times - 1)
        + chunk_scratch(utts, times, tail_rows),
        compiler_params=pltpu.CompilerParams(
            vmem_limit_bytes=VMEM_LIMIT, collective_id=1, has_side_effects=True
        ),
        cost_estimate=pl.CostEstimate(flops=40_000_000_000, bytes_accessed=30_000_000, transcendentals=0),
    )(
        lengths_row, *vecs, *tail, gtwo, gproj, hat_norm, scale_norm, hat_two, act, hat_one, scales, xin, embedded,
        wc1, tw, wc2, wsk, wh,
    )


def unpack_kernel(gnoisy, gmean, gtime, early_ref, middle_ref, late_ref, tail_ref, gseg_all_ref, time_all_ref, *refs):
    count = len(GRAD_SHAPES)
    finals, large, sem = refs[3 : count + 3], refs[count + 3 : -1], refs[-1]
    copies = []

    def send(source, target):
        copies.append(pltpu.make_async_copy(source, target, sem.at[len(copies)]))
        copies[-1].start()

    for source, target in zip((gnoisy, gmean, gtime), refs[0:3]):
        send(source, target)
    staged = dict(zip(LARGE_GRADS, large))
    outs = [staged.get(index, ref) for index, ref in enumerate(finals)]
    (
        gwc1, gb1, gg1, gs1, gtw, gtb, gwc2, gb2, gg2, gs2, gwsk, gsb, gng, gns, gwh, gwo, gob, gfg, gfs, gwe, geb, gsa,
        gsbeta, gwr, grb, gwd, gdb,
    ) = outs
    f32 = jnp.float32
    for tap in range(3):
        gwc1[tap] = late_ref[160 * tap : 160 * tap + 160, :].astype(f32)
        gwc2[tap] = middle_ref[256 * tap : 256 * tap + 256, :].astype(f32)
        gwd[tap] = tail_ref[256 * tap : 256 * tap + 256, :].astype(f32)
    gwh[...] = early_ref[0:384, :].astype(f32).T
    gwsk[0:128, :] = early_ref[384:512, :].astype(f32)
    gwsk[128:160, :] = middle_ref[768:800, :].astype(f32)
    rows = late_ref[480:496, :].astype(f32)
    for at, ref in enumerate((gng, gns, gsb, gg2, gs2, gb2, gg1, gs1, gb1)):
        ref[...] = rows[at : at + 1]
    half = time_all_ref.shape[1]
    time_cols = time_all_ref[...].T
    seg_rows = gseg_all_ref[...].astype(f32)
    low_half = lax.broadcasted_iota(jnp.int32, seg_rows.shape, 0) % 16 < 8
    swapped = jnp.concatenate([seg_rows[8:], seg_rows[0:8]], axis=0)
    behind = jnp.concatenate([seg_rows[-8:], seg_rows[0:-8]], axis=0)
    zero = jnp.zeros_like(seg_rows)
    first = jnp.concatenate([jnp.where(low_half, seg_rows, zero), jnp.where(low_half, swapped, zero)], axis=1)
    second = jnp.concatenate([jnp.where(low_half, zero, behind), jnp.where(low_half, zero, seg_rows)], axis=1)
    gtw[0:half, :] = dot(time_cols, first.astype(jnp.bfloat16))
    gtw[half:, :] = dot(time_cols, second.astype(jnp.bfloat16))
    gtb[...] = jnp.sum(first, axis=0, keepdims=True)
    gwr[...] = tail_ref[768:1792, :].astype(f32)
    for index in (0, 4, 6, 10, 14, 25):
        send(staged[index], finals[index])
    gwe[...] = tail_ref[1792:2816, :].astype(f32).T
    gwo[...] = tail_ref[2816:2944, :].astype(f32)
    for index in (15, 19, 23):
        send(staged[index], finals[index])
    rows = tail_ref[2944:2976, :].astype(f32)
    for at, ref in enumerate((gdb, grb, gfg, gfs, gob)):
        ref[...] = rows[at : at + 1]
    for at, ref in enumerate((geb, gsa, gsbeta)):
        for part in range(4):
            ref[:, 256 * part : 256 * part + 256] = rows[5 + 4 * at + part : 6 + 4 * at + part]
    for copy in copies:
        copy.wait()


GRAD_SHAPES = (
    (3, 160, 256), (1, 256), (1, 256), (1, 256), (1024, 256), (1, 256), (3, 256, 256), (1, 256), (1, 256), (1, 256),
    (160, 256), (1, 256), (1, 256), (1, 256), (256, 384), (128, 256), (1, 256), (1, 256), (1, 256), (256, 1024),
    (1, 1024), (1, 1024), (1, 1024), (1024, 256), (1, 256), (3, 256, 256), (1, 256),
)


LARGE_GRADS = (0, 4, 6, 10, 14, 15, 19, 23, 25)


def unpack_grads(gnoisy, gmean, gtime, *packed):
    carried = tuple(jax.ShapeDtypeStruct(item.shape, item.dtype) for item in (gnoisy, gmean, gtime))
    shapes = tuple(jax.ShapeDtypeStruct(shape, jnp.float32) for shape in GRAD_SHAPES)
    specs = tuple(ANYWHERE if index in LARGE_GRADS else WHOLE for index in range(len(GRAD_SHAPES)))
    outs = pl.pallas_call(
        unpack_kernel,
        name="unpack_grads",
        out_shape=carried + shapes,
        in_specs=[WHOLE] * (3 + len(packed)),
        out_specs=(ANYWHERE,) * 3 + specs,
        scratch_shapes=[pltpu.VMEM(GRAD_SHAPES[index], jnp.float32) for index in LARGE_GRADS]
        + [pltpu.SemaphoreType.DMA((3 + len(LARGE_GRADS),))],
        compiler_params=PARAMS,
    )(gnoisy, gmean, gtime, *packed)
    grads = tuple(out.reshape(out.shape[1]) if out.shape[0] == 1 else out for out in outs[3:])
    return (outs[0][None], outs[1], outs[2][None]) + grads


TAIL_ROWS = 2976


def shards(
    utts,
    times,
    noisy_mel,
    encoder_mean,
    time_embedding,
    utter_lengths,
    out_cotangent,
    conv_one,
    bias_one,
    gain_one,
    shift_one,
    time_weight,
    time_bias,
    conv_two,
    bias_two,
    gain_two,
    shift_two,
    skip_weight,
    skip_bias,
    norm_gain,
    norm_shift,
    heads_input,
    heads_output,
    output_bias,
    feed_gain,
    feed_shift,
    expand_weight,
    expand_bias,
    snake_alpha,
    snake_beta,
    reduce_weight,
    reduce_bias,
    down_weight,
    down_bias,
):
    lengths_row = utter_lengths[0]
    noisy = noisy_mel[0]
    embedded = time_embedding[0]
    vecs_res = (
        bias_one, gain_one, shift_one, time_bias, bias_two, gain_two, shift_two, skip_bias, norm_gain, norm_shift
    )
    hat_one, act, hat_two, hat_norm, scale_norm, resid_one, projected, scales, xin, time_all = res_forward(
        utts, times, lengths_row, vecs_res, noisy, encoder_mean, embedded, conv_one, time_weight, conv_two, skip_weight, heads_input
    )
    attended, log_sums = attention_forward(projected, lengths_row)
    down_output, grad_two, grad_attended, *tail = feed_forward(
        utts, times, padded_rows(TAIL_ROWS, utts, times), lengths_row, (output_bias, feed_gain, feed_shift, reduce_bias, down_bias),
        (expand_bias, snake_alpha, snake_beta), resid_one, attended, out_cotangent[0],
        heads_output, expand_weight, reduce_weight, down_weight,
    )
    tail = tail[0:1] + [
        lax.ppermute(chunk, ("utt", "tm"), chunk_moves(utts, times, step + 1)) for step, chunk in enumerate(tail[1:])
    ]
    grad_projected = attention_backward(projected, attended, log_sums, grad_attended, lengths_row)
    grad_noisy, grad_mean, grad_time, *packed = res_backward(
        utts, times, lengths_row, vecs_res, grad_two, grad_projected, hat_norm, scale_norm, hat_two, act, hat_one,
        scales, xin, embedded, conv_one, time_weight, conv_two, skip_weight, heads_input, tail,
    )
    return (down_output[None],) + unpack_grads(grad_noisy, grad_mean, grad_time, *packed, time_all)


def solution(mesh):
    return jax.shard_map(
        functools.partial(shards, mesh.shape["utt"], mesh.shape["tm"]),
        mesh=mesh,
        in_specs=(
            P("tm", None, "utt"),
            P(None, ("utt", "tm")),
            P("tm", "utt", None),
            P("utt", None),
            P("tm", None, "utt"),
            P(),
            P(),
            P(),
            P(),
            P(),
            P(),
            P(),
            P(),
            P(),
            P(),
            P(),
            P(),
            P(),
            P(),
            P(),
            P(),
            P(),
            P(),
            P(),
            P(),
            P(),
            P(),
            P(),
            P(),
            P(),
            P(),
            P(),
        ),
        out_specs=(
            P("tm", None, "utt"),
            P("tm", None, "utt"),
            P(None, ("utt", "tm")),
            P("tm", "utt", None),
            P(),
            P(),
            P(),
            P(),
            P(),
            P(),
            P(),
            P(),
            P(),
            P(),
            P(),
            P(),
            P(),
            P(),
            P(),
            P(),
            P(),
            P(),
            P(),
            P(),
            P(),
            P(),
            P(),
            P(),
            P(),
            P(),
            P(),
        ),
        check_vma=False,
    )
```

time: 1160 us -> 239 us (0.21); the launches traced: 1140 us -> 238 us
  matrix products: 332 us -> 0 us
  blocking collectives: 312 us -> 0 us
  Pallas kernels: 0 us -> 232 us
  local copies, waits for them, and re-layouts: 187 us -> 0.97 us
  other arithmetic: 104 us -> 0 us
  loops' own time: 97 us -> 0 us
  waiting for transfers between devices: 92.7 us -> 0.01 us
  between operations: 18.8 us -> 0.91 us
    dot_general x157 -> x0, matrix products: 332 us -> none  [the longest x14 103 us: input_grad(): return jnp.dot(weight, grad_low, preferred_element_type=jnp.float32)]
    psum x1 -> x0, blocking collectives: 300 us -> none  [sum_head(): lax.psum((parts[0], parts[1], parts[2], parts[3], parts[4], parts[5], par...]
    pallas_call x0 -> x6, Pallas kernels: none -> 232 us  [the longest x1 97.3 us: res_backward(): pl.pallas_call(functools.partial(res_backward_kernel, lengths_row.shape[0...]
    another operation x20 -> x0, loops' own time: 97 us -> none  [the longest x1 47.4 us: attention_forward(): return lax.fori_loop(0, block_count, one_block, start_carry)]
    psum x1 -> x0, waiting for transfers between devices: 92.7 us -> none  [sum_head(): lax.psum((parts[0], parts[1], parts[2], parts[3], parts[4], parts[5], par...]
    slice x13 -> x0, local copies, waits for them, and re-layouts: 84 us -> none  [the longest x1 37.5 us: down_taps(): even_cols = inputs[:, 0::2]]
    reduce_sum x54 -> x0, other arithmetic: 70.8 us -> none  [the longest x9 20.1 us: segment_spread(): return jnp.sum(statistic[:, :, None] * seg_rows[None], axis=1)]
    dynamic_slice x114 -> x0, local copies, waits for them, and re-layouts: 37.4 us -> none  [the longest x24 14.2 us: key_range(): key_high = (ends_at[segment[last]] + block - 1) // block]
  transfers between devices with their start and end apart: 2 -> 3, of which waited for: 1 -> 0; matrix products, arithmetic and copies ran while one was open for 12% -> 0% of each run, Pallas kernels for 0% -> 12%
where the time goes in v1:
time: 239 us; the launch traced here: 238 us
  Pallas kernels  232 us (97%)
  starting transfers between devices  3.6 us (2%)
    pallas_call x1, Pallas kernels, res_backward(): pl.pallas_call(functools.partial(res_backward_kernel, lengths_row.shape[0...  97.3 us
    pallas_call x1, Pallas kernels, feed_forward(): pl.pallas_call(functools.partial(ffn_kernel, lengths_row.shape[0], utts,...  46.4 us
    pallas_call x1, Pallas kernels, res_forward(): pl.pallas_call(functools.partial(res_forward_kernel, lengths_row.shape[0]...  36.6 us
    pallas_call x1, Pallas kernels, attention_backward(): pl.pallas_call(functools.partial(attn_backward_kernel, segs), name='atten...  28.5 us
    pallas_call x1, Pallas kernels, attention_forward(): pl.pallas_call(functools.partial(attn_forward_kernel, segs), name='attent...  17.3 us
    pallas_call x1, Pallas kernels, unpack_grads(): pl.pallas_call(unpack_kernel, name='unpack_grads', out_shape=carried + sh...  6.46 us
  transfers between devices with their start and end apart: 3, of which 0 were waited for; matrix products, arithmetic and copies ran while one was open for 0% of the time, Pallas kernels for 12%

profile of v1, /device:TPU:0, one launch (start us, length us, event | category | flops | bytes accessed | tf_op | source)
XLA Modules:
  0.0 237.9 jit_solution(16152624768783809262)
XLA Ops:
  0.7 36.6 %res_forward.1 = (bf16[256,4096]{1,0:T(8,128)(2,1)}, bf16[256,4096]{1,0:T(8,128)(2,1)}, bf16[256,4096]{1,0:T(8,128)(2,1)}, bf16[256,4096]{1,0:T(8,128)(2,1)}, f3...) custom-call(s32[8]{0:T(128)} %bitcast.29, ...), custom_call_target="tpu_custom_call" | custom-call | tf_op jit(solution)/shard_map/res_forward/pallas_call | solution.py:1335
  37.3 17.3 %attention_forward.1 = (f32[128,4096]{1,0:T(8,128)}, f32[8,4096]{1,0:T(8,128)}) custom-call(s32[8]{0:T(128)} %bitcast.30, bf16[384,4096]{1,0:T(8,128)(2,1)} %get-tuple-element.89.proj_ref), custom_call_target="tpu_custom_call" | custom-call | tf_op jit(solution)/shard_map/attention_forward/pallas_call | solution.py:290
  54.5 46.4 %feed_forward.1 = (bf16[256,2048]{1,0:T(8,128)(2,1)}, f32[256,4096]{1,0:T(8,128)}, bf16[128,4096]{1,0:T(8,128)(2,1)}, bf16[768,256]{1,0:T(8,128)(2,1)}, bf16[768...) custom-call(s32[8]{0:T(128)} %bitcast.31, bf16[256]{0:T(256)(128)(2,1)} %refs_0_.4, ...), custom_call_target="tpu_custom_call" | custom-call | tf_op jit(solution)/shard_map/feed_forward/pallas_call | solution.py:644
  100.9 2.1 collective-permute-start
  103.0 0.0 collective-permute-start.1
  103.0 1.5 collective-permute-start.2
  104.5 28.5 %attention_backward.1.refs_15_ = bf16[384,4096]{1,0:T(8,128)(2,1)} custom-call(s32[8]{0:T(128)} %bitcast.32, bf16[384,4096]{1,0:T(8,128)(2,1)} %get-tuple-element.89.proj_ref, f32[128,4096]{1,0:T(8,128)} %get-tuple-element.90.refs_9_.att_ref, f32[8,4096]{1,0:T(8,128)} %get-tuple-element.97.lse_ref, bf16[128,4096]{1,0:T(8,128)(2,1)} %get-tuple-element.98.gatt_ref), custom_call_target="tpu_custom_call" | custom-call | flops 40000000000 | bytes 10000000 | tf_op jit(solution)/shard_map/attention_backward/pallas_call | solution.py:311
  133.0 0.0 collective-permute-done.refs_11_
  133.0 0.0 copy-start
  133.0 0.0 collective-permute-done.1.refs_12_
  133.0 0.0 copy-start.1
  133.0 0.0 collective-permute-done.2.refs_13_
  133.0 0.0 copy-start.2
  133.0 0.7 copy-done
  133.7 0.1 copy-done.1
  133.9 0.1 copy-done.2
  134.0 97.3 %res_backward.1 = (f32[80,4096]{1,0:T(8,128)}, f32[80,2048]{1,0:T(8,128)}, f32[8,1024]{1,0:T(8,128)}, bf16[512,256]{1,0:T(8,128)(2,1)}, bf16[1024,256]{1,0:T(8,1...) custom-call(s32[8]{0:T(128)} %bitcast.33, bf16[256]{0:T(256)(128)(2,1)} %refs_0_.5, ...), custom_call_target="tpu_custom_call" | custom-call | flops 40000000000 | bytes 30000000 | tf_op jit(solution)/shard_map/res_backward/pallas_call | solution.py:1694
  231.3 6.5 %unpack_grads.1 = (f32[80,4096]{1,0:T(8,128)}, f32[80,2048]{1,0:T(8,128)}, f32[8,1024]{1,0:T(8,128)}, f32[3,160,256]{2,1,0:T(8,128)}, f32[1,256]{1,0:T(1,128)}, ...) custom-call(f32[80,4096]{1,0:T(8,128)} %get-tuple-element.106.gnoisy, ...), custom_call_target="tpu_custom_call" | custom-call | tf_op jit(solution)/shard_map/unpack_grads/pallas_call | solution.py:1826
Async XLA Ops:
  100.9 32.1 %collective-permute-start = (bf16[768,256]{1,0:T(8,128)(2,1)}, bf16[768,256]{1,0:T(8,128)(2,1)S(1)}, u32[]{:S(2)}, u32[]{:S(2)}) collective-permute-start(bf16[768,256]{1,0:T(8,128)(2,1)} %get-tuple-element.93), channel_id=1, source_target_pairs={{0,1},{1,4},{4,5},{5,0},{2,3},{3,6},{6,7},{7,2},{8,9},{9,12},{12,1... | collective-permute-start | bytes 1179656 | tf_op jit(solution)/shard_map/ppermute | solution.py:1895
  103.0 30.0 %collective-permute-start.1 = (bf16[768,256]{1,0:T(8,128)(2,1)}, bf16[768,256]{1,0:T(8,128)(2,1)S(1)}, u32[]{:S(2)}, u32[]{:S(2)}) collective-permute-start(bf16[768,256]{1,0:T(8,128)(2,1)} %get-tuple-element.94), channel_id=1, source_target_pairs={{0,4},{1,5},{4,0},{5,1},{2,6},{3,7},{6,2},{7,3},{8,12},{9,13},{12,... | collective-permute-start | bytes 1179656 | tf_op jit(solution)/shard_map/ppermute | solution.py:1895
  103.0 30.0 %collective-permute-start.2 = (bf16[768,256]{1,0:T(8,128)(2,1)}, bf16[768,256]{1,0:T(8,128)(2,1)S(1)}, u32[]{:S(2)}, u32[]{:S(2)}) collective-permute-start(bf16[768,256]{1,0:T(8,128)(2,1)} %get-tuple-element.95), channel_id=1, source_target_pairs={{0,5},{1,0},{4,1},{5,4},{2,7},{3,2},{6,3},{7,6},{8,13},{9,8},{12,9... | collective-permute-start | bytes 1179656 | tf_op jit(solution)/shard_map/ppermute | solution.py:1895
  133.0 0.7 copy-start
  133.0 0.9 copy-start.1
  133.0 1.0 copy-start.2
